TPU v7x, 512 devices: a whole 4x4x16 slice. The times are simulated.
512 devices in a mesh: patch: 32 (over z, core), tensor: 8 (over y, x_lo), guidance: 2 (over x_hi).
Axes of the slice: x: 4 (x_hi: 2, x_lo: 2; x = x_hi * 2 + x_lo), y: 4, z: 16, core: 2. Of those that a mesh axis runs over, the one named last changes fastest.
Arguments:
- tokens: bfloat16 [4096, 3072], P('patch', 'tensor'), may hold values from -6 to 6
- modulation: float32 [3, 2, 3072], replicated, may hold values from -3 to 3
- w_qkv: bfloat16 [3, 3072, 2048], P(None, None, ('tensor', 'guidance')), may hold values from -0.109375 to 0.109375
- w_out: bfloat16 [2048, 3072], P(('tensor', 'guidance')), may hold values from -6 to 6
- stale: bfloat16 [2, 2, 4096, 2048], P(None, 'guidance', 'patch', 'tensor'), may hold values from -48 to 48
- text: bfloat16 [2, 2, 256, 2048], P(None, 'guidance', None, 'tensor'), may hold values from -6 to 6
Outputs:
- mixed: bfloat16 [4096, 3072], P('patch', 'tensor')
All inputs are finite; a program needn't handle non-finite values.
Results may differ from a plain program's by a relative error of at most 0.02.
Values may be sent and summed in bfloat16 or wider, within the bound.
No kernel may reach another device: no remote copies, remote signals or barrier semaphores. Data moves between devices by JAX's collectives and lax.ppermute only.
A program may use at most 64 MiB of HBM per device.

v0:
```python
import math

import jax
import jax.numpy as jnp
from jax import lax
from jax.sharding import PartitionSpec as P

HEAD = 128


GUIDE = 3.0
EPSILON = 1e-06
NEGATIVE = -1e30


def head_normalize(projected, head_size):
    shaped = projected.reshape(projected.shape[:-1] + (projected.shape[-1] // head_size, head_size))
    scaled = shaped * lax.rsqrt(jnp.mean(shaped * shaped, axis=-1, keepdims=True) + EPSILON)
    return scaled.reshape(projected.shape).astype(jnp.bfloat16)


def finish_projection(projected, head_size):
    return jnp.stack(
        [
            head_normalize(projected[..., 0, :, :], head_size),
            head_normalize(projected[..., 1, :, :], head_size),
            projected[..., 2, :, :].astype(jnp.bfloat16),
        ],
        axis=-3,
    )


def attend_block(state_tuple, queries, block_keys, block_values, allowed):
    running_max, running_sum, running_acc = state_tuple
    scores = jnp.einsum(
        "thd,khd->htk", queries, block_keys, preferred_element_type=jnp.float32
    ) * queries.shape[-1] ** (-0.5)
    if allowed is not None:
        scores = jnp.where(allowed[None, None, :], scores, NEGATIVE)
    new_max = jnp.maximum(running_max, jnp.max(scores, axis=-1))
    rescale = jnp.exp(running_max - new_max)
    weights = jnp.exp(scores - new_max[..., None])
    new_sum = running_sum * rescale + jnp.sum(weights, axis=-1)
    new_acc = running_acc * rescale[..., None] + jnp.einsum(
        "htk,khd->htd",
        weights.astype(jnp.bfloat16),
        block_values,
        preferred_element_type=jnp.float32,
    )
    return (new_max, new_sum, new_acc)


def local(tokens, modulation, w_qkv, w_out, stale, text):
    branch_index = lax.axis_index("guidance")
    patch_index = lax.axis_index("patch")
    row_count = tokens.shape[0]
    head_size = HEAD
    gathered = lax.all_gather(tokens, "tensor", axis=1, tiled=True)
    tokens_f32 = gathered.astype(jnp.float32)
    average = jnp.mean(tokens_f32, axis=-1, keepdims=True)
    centered = tokens_f32 - average
    normed = centered * lax.rsqrt(jnp.mean(centered * centered, axis=-1, keepdims=True) + EPSILON)
    shift = lax.dynamic_index_in_dim(modulation[0], branch_index, 0, keepdims=False)
    scale = lax.dynamic_index_in_dim(modulation[1], branch_index, 0, keepdims=False)
    modulated = (normed * (1.0 + scale) + shift).astype(jnp.bfloat16)
    product = jnp.einsum(
        "td,kdc->ktc",
        modulated,
        lax.all_gather(w_qkv, "guidance", axis=2, tiled=True),
        preferred_element_type=jnp.float32,
    )
    prepared = finish_projection(product, head_size)
    local_heads = prepared.shape[-1] // head_size
    queries = prepared[0].reshape(row_count, local_heads, head_size)
    fresh_keys = prepared[1].reshape(row_count, local_heads, head_size)
    fresh_values = prepared[2].reshape(row_count, local_heads, head_size)
    text_keys = text[0, 0].reshape(text.shape[2], local_heads, head_size)
    text_values = text[1, 0].reshape(text.shape[2], local_heads, head_size)
    initial = (
        jnp.full((local_heads, row_count), NEGATIVE, jnp.float32),
        jnp.zeros((local_heads, row_count), jnp.float32),
        jnp.zeros((local_heads, row_count, head_size), jnp.float32),
    )
    state_tuple = attend_block(
        initial,
        queries,
        jnp.concatenate([text_keys, fresh_keys], axis=0),
        jnp.concatenate([text_values, fresh_values], axis=0),
        None,
    )
    own_first = patch_index * row_count
    stale_piece = lax.all_gather(stale, "patch", axis=2, tiled=True)
    piece_rows = stale_piece.shape[2]
    block_rows = math.gcd(piece_rows, 1024)
    block_count = piece_rows // block_rows
    key_blocks = stale_piece[0, 0].reshape(block_count, block_rows, local_heads, head_size)
    value_blocks = stale_piece[1, 0].reshape(block_count, block_rows, local_heads, head_size)
    offsets = jnp.arange(block_count, dtype=jnp.int32) * block_rows

    def step_block(inner_state, inputs):
        block_keys, block_values, offset = inputs
        positions = offset + jnp.arange(block_rows, dtype=jnp.int32)
        allowed = (positions < own_first) | (positions >= own_first + row_count)
        return (attend_block(inner_state, queries, block_keys, block_values, allowed), None)

    final_state, unused = lax.scan(step_block, state_tuple, (key_blocks, value_blocks, offsets))
    state_tuple = final_state
    final_max, final_sum, final_acc = state_tuple
    attended = (
        (final_acc / final_sum[..., None])
        .transpose(1, 0, 2)
        .reshape(row_count, local_heads * head_size)
        .astype(jnp.bfloat16)
    )
    branch_out = jnp.dot(
        attended,
        lax.all_gather(w_out, "guidance", axis=0, tiled=True),
        preferred_element_type=jnp.float32,
    )
    coefficient = jnp.where(branch_index == 0, GUIDE, 1.0 - GUIDE)
    contributions = (
        coefficient
        * lax.dynamic_index_in_dim(modulation[2], branch_index, 0, keepdims=False)
        * branch_out
    )
    partial_sum = lax.psum_scatter(
        contributions.astype(jnp.bfloat16), "tensor", scatter_dimension=1, tiled=True
    )
    guided = lax.psum(partial_sum, "guidance").astype(jnp.float32)
    return (tokens.astype(jnp.float32) + guided).astype(jnp.bfloat16)


def solution(mesh):
    in_specs = (
        P("patch", "tensor"),
        P(),
        P(None, None, ("tensor", "guidance")),
        P(("tensor", "guidance"), None),
        P(None, "guidance", "patch", "tensor"),
        P(None, "guidance", None, "tensor"),
    )
    out_specs = P("patch", "tensor")
    return jax.shard_map(local, mesh=mesh, in_specs=in_specs, out_specs=out_specs, check_vma=False)
```

profile of v0, /device:TPU:1, one launch (start us, length us, event | category | flops | bytes accessed | tf_op | source)
XLA Modules:
  0.0 308.7 jit_solution(7401094813494660955)
XLA Ops:
  6.5 0.7 all-gather.4.cloned.1.call-update
  7.3 0.0 all-gather.6.cloned.1.call-start
  7.3 0.7 all-gather.6.cloned.1.call-update
  8.0 0.0 all-gather.8.cloned.1.call-start
  8.1 0.7 all-gather.8.cloned.1.call-update
  8.8 0.0 reduce-scatter.4.cloned.1.call-start
  8.9 26.9 %all_gather.12 = bf16[128,3072]{1,0:T(8,128)(2,1)S(1)} all-gather(bf16[128,384]{1,0:T(8,128)(2,1)S(1)} %copy-done), channel_id=1, replica_groups=mesh['patch'=32,'tensor'=8,'guidance'=2] {'tensor'}, dimensions={1}, use_global_device_ids=true | all-gather | bytes 884736 | tf_op jit(solution)/shard_map/all_gather | solution.py:58
  35.8 0.2 convert_reduce_fusion
  36.0 0.4 fusion.12
  36.4 0.1 copy.53
  36.5 0.1 copy.41
  36.6 0.1 copy.54
  36.7 0.1 copy.43
  36.9 53.2 %all-gather.4.cloned.1.call-done = bf16[3,3072,256]{2,1,0:T(8,128)(2,1)} async-done(((bf16[3,3072,128]{2,1,0:T(8,128)(2,1)}), bf16[3,3072,256]{2,1,0:T(8,128)(2,1)}) %all-gather.4.cloned.1.call-update) | async-done | bytes 4718608 | tf_op jit(solution)/shard_map/all_gather | solution.py:69
  90.2 3.2 %convolution_bitcast_fusion = f32[3,128,256]{2,1,0:T(8,128)S(1)} fusion(bf16[3,3072,256]{2,1,0:T(8,128)(2,1)} %all-gather.4.cloned.1.call-done, bf16[128,3072]{1,0:T(8,128)(2,1)S(1)} %all_gather.12, f32[3072]{0:T(1024)S(1)} %bitcast.50, f32[3072]{0:T(1024)S(1)} %bitcast.49, f32[128]{0:T(128)S(1)} %add_rsqrt_fusion.2, f32[128]{0:T(128)S(1)} %broadcast_multiply_fusion), kind=kOutput, calls=%fused_computation.29 | convolution fusion | flops 606339072 | bytes 5923840 | tf_op jit(solution)/shard_map/td,kdc->ktc/dot_general | solution.py:66
  93.4 0.1 reshape_squeeze.18
  93.5 0.2 multiply_reduce_fusion.1
  93.7 0.1 copy.36
  93.8 0.1 fusion.33
  93.9 0.1 reshape_squeeze.20
  94.0 0.2 multiply_reduce_fusion
  94.2 0.1 copy.39
  94.3 0.1 fusion.32
  94.4 0.3 fusion.42
  94.7 0.2 fusion.23
  95.0 0.3 convolution_add_fusion.1
  95.3 71.8 %all-gather.6.cloned.1.call-done = bf16[2,1,4096,256]{3,2,1,0:T(8,128)(2,1)} async-done(((bf16[2,1,128,256]{3,2,1,0:T(8,128)(2,1)}), bf16[2,1,4096,256]{3,2,1,0:T(8,128)(2,1)}) %all-gather.6.cloned.1.call-update) | async-done | bytes 4194320 | tf_op jit(solution)/shard_map/all_gather | solution.py:92
  167.1 4.5 %fusion.38 = (bf16[1,1,4096,256]{3,2,1,0:T(8,128)(2,1)}, bf16[1,1,4096,256]{3,2,1,0:T(8,128)(2,1)}) fusion(bf16[2,1,4096,256]{3,2,1,0:T(8,128)(2,1)} %all-gather.6.cloned.1.call-done), kind=kLoop, calls=%fused_computation.69 | loop fusion | bytes 8388608 | tf_op jit(solution)/shard_map/slice | solution.py:97
  171.6 2.5 reshape_squeeze.22
  174.1 4.0 %reshape_squeeze.23 = bf16[4,1024,2,128]{3,2,1,0:T(2,128)(2,1)} reshape(bf16[1,1,4096,256]{3,2,1,0:T(8,128)(2,1)} %get-tuple-element.152) | data formatting | bytes 4194304 | tf_op jit(solution)/shard_map/reshape;squeeze | solution.py:97
  178.1 18.4 %while.15 = (s32[]{:T(128)}, f32[2,128]{1,0:T(2,128)S(1)}, f32[2,128]{1,0:T(2,128)S(1)}, f32[2,128,128]{2,1,0:T(8,128)S(1)}, s32[4]{0:T(128)S(1)}, /*index=5*/s3...) while((s32[]{:T(128)}, f32[2,128]{1,0:T(2,128)S(1)}, ...), condition=%wide.region_9.10_spmd, body=%wide.region_6.9_spmd.sunk | while | flops 136122880 | bytes 6637705 | solution.py:106
  178.1 1.8 constant_dynamic-slice_fusion.4
  179.9 0.6 dynamic_slice.35
  180.5 0.6 fusion.55
  181.1 1.0 fusion.56
  182.1 0.2 fusion.57
  182.3 0.4 convolution_add_fusion.3
  182.7 1.8 constant_dynamic-slice_fusion.4
  184.5 0.6 dynamic_slice.35
  185.1 0.6 fusion.55
  185.7 1.0 fusion.56
  186.7 0.2 fusion.57
  186.9 0.4 convolution_add_fusion.3
  187.3 1.8 constant_dynamic-slice_fusion.4
  189.1 0.6 dynamic_slice.35
  189.7 0.6 fusion.55
  190.3 1.0 fusion.56
  191.3 0.2 fusion.57
  191.5 0.4 convolution_add_fusion.3
  191.9 1.8 constant_dynamic-slice_fusion.4
  193.7 0.6 dynamic_slice.35
  194.3 0.6 fusion.55
  194.9 1.0 fusion.56
  195.9 0.2 fusion.57
  196.1 0.4 convolution_add_fusion.3
  196.5 0.1 copy.47
  196.7 8.2 %all-gather.8.cloned.1.call-done = bf16[256,3072]{1,0:T(8,128)(2,1)} async-done(((bf16[128,3072]{1,0:T(8,128)(2,1)}), bf16[256,3072]{1,0:T(8,128)(2,1)}) %all-gather.8.cloned.1.call-update) | async-done | bytes 1572880 | tf_op jit(solution)/shard_map/all_gather | solution.py:117
  204.9 1.8 fusion.9
  206.7 1.2 copy.49
  207.9 0.0 all-reduce.2.cloned.1.call-start
  207.9 42.1 %reduce-scatter.4.cloned.1.call-done = bf16[384,128]{1,0:T(8,128)(2,1)} async-done(((bf16[3072,128]{1,0:T(8,128)(2,1)}), bf16[384,128]{1,0:T(8,128)(2,1)}) %reduce-scatter.4.cloned.1.call-update) | async-done | bytes 98320
  250.0 1.6 copy.50
  251.7 48.9 %all-reduce.2.cloned.1.call-done = bf16[128,384]{1,0:T(8,128)(2,1)} async-done(((bf16[128,384]{1,0:T(8,128)(2,1)}), bf16[128,384]{1,0:T(8,128)(2,1)}) %all-reduce.2.cloned.1.call-update) | async-done | bytes 98320 | tf_op jit(solution)/shard_map/psum | solution.py:129
  300.6 1.6 add_convert_fusion
  (37 shorter events, 0.3 us)
Async XLA Ops:
  6.5 2.3 copy-start.2
  6.5 2.3 copy-start
  6.5 83.6 %all-gather.4.cloned.1.call-start = ((), (), s32[]{:S(2)}) async-start(), calls=%async_computation.1 | async-start | bytes 7077888 | tf_op jit(solution)/shard_map/all_gather | solution.py:69
  7.3 159.9 %all-gather.6.cloned.1.call-start = ((), (), s32[]{:S(2)}) async-start(), calls=%async_computation.2 | async-start | bytes 4325376 | tf_op jit(solution)/shard_map/all_gather | solution.py:92
  8.0 28.3 %copy-start.1 = (bf16[2,1,256,256]{3,2,1,0:T(8,128)(2,1)S(1)}, bf16[2,1,256,256]{3,2,1,0:T(8,128)(2,1)}, u32[]{:S(2)}) copy-start(bf16[2,1,256,256]{3,2,1,0:T(8,128)(2,1)} %param.13) | copy-start | bytes 786436
  8.0 196.8 %all-gather.8.cloned.1.call-start = ((), (), s32[]{:S(2)}) async-start(), calls=%async_computation.3 | async-start | bytes 2359296 | tf_op jit(solution)/shard_map/all_gather | solution.py:117
  8.8 241.3 %reduce-scatter.4.cloned.1.call-start = ((), (), s32[]{:S(2)}) async-start(), calls=%async_computation.5 | async-start | bytes 884736
  207.9 92.7 %all-reduce.2.cloned.1.call-start = ((), (), s32[]{:S(2)}) async-start(), calls=%async_computation.4 | async-start | bytes 196608 | tf_op jit(solution)/shard_map/psum | solution.py:129
Sparse Core Ops, SparseCore 0:
  9.4 80.6 all-gather.3
  92.3 74.7 all-gather.5
  169.2 35.6 all-gather.7
  208.0 42.0 reduce-scatter.3
  253.0 47.5 all-reduce.1
where the time goes:
time: 309 us
  waiting for transfers between devices  226 us (73%)
  blocking collectives  26.9 us (9%)
  local copies, waits for them, and re-layouts  24.2 us (8%)
  between operations  13.4 us (4%)
  matrix products  11.1 us (4%)
  other arithmetic  6.32 us (2%)
    all_gather x1, waiting for transfers between devices, local(): stale_piece = lax.all_gather(stale, 'patch', axis=2, tiled=True)  71.8 us
    all_gather x1, waiting for transfers between devices, local(): lax.all_gather(w_qkv, 'guidance', axis=2, tiled=True)  53.2 us
    psum x1, waiting for transfers between devices, local(): guided = lax.psum(partial_sum, 'guidance').astype(jnp.float32)  48.9 us
    unnamed x6, waiting for transfers between devices  44.3 us
    all_gather x1, blocking collectives, local(): gathered = lax.all_gather(tokens, 'tensor', axis=1, tiled=True)  26.9 us
    dynamic_slice x8, local copies, waits for them, and re-layouts, local(): lax.scan(step_block, state_tuple, (key_blocks, value_blocks, offsets))  9.49 us
    all_gather x1, waiting for transfers between devices, local(): lax.all_gather(w_out, 'guidance', axis=0, tiled=True)  8.21 us
  transfers between devices with their start and end apart: 5, of which 5 were waited for; matrix products, arithmetic and copies ran while one was open for 11% of the time, Pallas kernels for 0%

commit v1 on v0

v1 whole, which is shorter than its diff:
```python
import math

import jax
import jax.numpy as jnp
from jax import lax
from jax.experimental import pallas as pl
from jax.experimental.pallas import tpu as pltpu
from jax.sharding import PartitionSpec as P

HEAD = 128
GUIDE = 3.0
EPSILON = 1e-06
NEGATIVE = -1e30
BASE = math.log2(math.e) / math.sqrt(HEAD)
BLOCK = 128
PARTS = 8
COLS = 384
SHARE = 4
FRESH = BLOCK // SHARE
ASK = BLOCK + 2 * FRESH
REPLY = 2 * BLOCK + 16
BF16 = jnp.bfloat16
F32 = jnp.float32
VMEM = 24 * 1024 * 1024


def nt(a, b):
    return lax.dot_general(a, b, (((1,), (1,)), ((), ())), preferred_element_type=F32)


def nn(a, b):
    return jnp.dot(a, b, preferred_element_type=F32)


def project_kernel(x_ref, mod_ref, w_ref, out_ref):
    total = jnp.zeros((BLOCK, 1), F32)
    for b in range(PARTS):
        total += jnp.sum(x_ref[b].astype(F32), axis=-1, keepdims=True)
    average = total * (1.0 / (PARTS * COLS))
    total = jnp.zeros((BLOCK, 1), F32)
    for b in range(PARTS):
        centered = x_ref[b].astype(F32) - average
        total += jnp.sum(centered * centered, axis=-1, keepdims=True)
    inverse = lax.rsqrt(total * (1.0 / (PARTS * COLS)) + EPSILON)
    sums = [jnp.zeros((2 * BLOCK, HEAD), F32) for _ in range(3)]
    for b in range(PARTS):
        cols = slice(b * COLS, (b + 1) * COLS)
        normed = (x_ref[b].astype(F32) - average) * inverse
        both = [
            (normed * (1.0 + mod_ref[1, p : p + 1, cols]) + mod_ref[0, p : p + 1, cols]).astype(BF16)
            for p in range(2)
        ]
        both = jnp.concatenate(both, axis=0)
        for i in range(3):
            sums[i] += nn(both, w_ref[i, cols, :])

    def head_norm(v):
        return (v * lax.rsqrt(jnp.mean(v * v, axis=-1, keepdims=True) + EPSILON)).astype(BF16)

    query, key, value = head_norm(sums[0]), head_norm(sums[1]), sums[2].astype(BF16)
    for p in range(2):
        for j in range(SHARE):
            d = p * SHARE + j
            rows = slice(p * BLOCK + j * FRESH, p * BLOCK + (j + 1) * FRESH)
            out_ref[d, 0:BLOCK, :] = query[p * BLOCK : (p + 1) * BLOCK]
            out_ref[d, BLOCK : BLOCK + FRESH, :] = key[rows]
            out_ref[d, BLOCK + FRESH : ASK, :] = value[rows]


def attend_kernel(ask_ref, kv0, kv1, kv2, kv3, text_ref, out_ref):
    own = lax.axis_index("za") * 2 + lax.axis_index("core")
    text_rows = text_ref.shape[1] // SHARE
    first = pl.multiple_of(own * text_rows, text_rows)
    query_rows = SHARE * BLOCK
    row_block = lax.broadcasted_iota(jnp.int32, (query_rows, 1), 0) // BLOCK
    col = lax.broadcasted_iota(jnp.int32, (1, 2 * BLOCK), 1)
    own_stale = (row_block == own) & (col < BLOCK)
    other_fresh = row_block != col[:, :BLOCK] // FRESH
    lane = lax.broadcasted_iota(jnp.int32, (1, HEAD), 1)
    stats = jnp.zeros((BLOCK, HEAD), F32)
    for h in range(2):
        cols = slice(h * HEAD, (h + 1) * HEAD)
        mine = slice(h * SHARE, (h + 1) * SHARE)
        query = ask_ref[mine, 0:BLOCK, :].reshape(query_rows, HEAD)
        scores, values = [], []
        for n, kv in enumerate((kv0, kv1, kv2, kv3)):
            s = nt(query, kv[:, 0, :, cols].reshape(2 * BLOCK, HEAD))
            if n == 0:
                s = jnp.where(own_stale, NEGATIVE, s)
            scores.append(s)
            values.append(kv[:, 1, :, cols].reshape(2 * BLOCK, HEAD))
        s = nt(query, ask_ref[mine, BLOCK : BLOCK + FRESH, :].reshape(BLOCK, HEAD))
        scores.append(jnp.where(other_fresh, NEGATIVE, s))
        values.append(ask_ref[mine, BLOCK + FRESH : ASK, :].reshape(BLOCK, HEAD))
        scores.append(nt(query, text_ref[0, pl.ds(first, text_rows), cols]))
        values.append(text_ref[1, pl.ds(first, text_rows), cols])
        top = jnp.max(scores[0], axis=-1, keepdims=True)
        for s in scores[1:]:
            top = jnp.maximum(top, jnp.max(s, axis=-1, keepdims=True))
        top = top * BASE
        total = jnp.zeros((query_rows, 1), F32)
        summed = jnp.zeros((query_rows, HEAD), F32)
        for s, v in zip(scores, values):
            weights = jnp.exp2(s * BASE - top)
            total += jnp.sum(weights, axis=-1, keepdims=True)
            summed += nn(weights.astype(BF16), v)
        summed = (summed / total).astype(BF16)
        level = top + jnp.log2(total)
        high = level.astype(BF16).astype(F32)
        middle = (level - high).astype(BF16).astype(F32)
        low = level - high - middle
        for b in range(SHARE):
            rows = slice(b * BLOCK, (b + 1) * BLOCK)
            for g in range(2):
                out_ref[g * SHARE + b, h * BLOCK : (h + 1) * BLOCK, :] = summed[rows]
            for i, piece in enumerate((high, middle, low)):
                stats = jnp.where(lane == 16 * b + 3 * h + i, piece[rows], stats)
    stats = jnp.transpose(stats).astype(BF16)
    for b in range(SHARE):
        for g in range(2):
            out_ref[g * SHARE + b, 2 * BLOCK : REPLY, :] = stats[16 * b : 16 * b + 16]


def output_kernel(reply_ref, mod_ref, w_ref, out_ref):
    stats = jnp.concatenate([reply_ref[s, 2 * BLOCK : REPLY, :].astype(F32) for s in range(2 * SHARE)], axis=0)
    stats = jnp.transpose(stats)
    attended = []
    for p in range(2):
        heads = []
        for h in range(2):
            levels = []
            for j in range(SHARE):
                c = 16 * (p * SHARE + j) + 3 * h
                levels.append(stats[:, c : c + 1] + stats[:, c + 1 : c + 2] + stats[:, c + 2 : c + 3])
            top = jnp.maximum(jnp.maximum(levels[0], levels[1]), jnp.maximum(levels[2], levels[3]))
            shares = [jnp.exp2(level - top) for level in levels]
            total = shares[0] + shares[1] + shares[2] + shares[3]
            summed = jnp.zeros((BLOCK, HEAD), F32)
            for j in range(SHARE):
                part = reply_ref[p * SHARE + j, h * BLOCK : (h + 1) * BLOCK, :].astype(F32)
                summed += shares[j] * part
            heads.append((summed / total).astype(BF16))
        attended.append(jnp.concatenate(heads, axis=1))
    attended = jnp.concatenate(attended, axis=0)
    for b in range(PARTS):
        cols = slice(b * COLS, (b + 1) * COLS)
        branch = nn(attended, w_ref[:, cols])
        mixed = (GUIDE * mod_ref[2, 0:1, cols]) * branch[:BLOCK]
        mixed += ((1.0 - GUIDE) * mod_ref[2, 1:2, cols]) * branch[BLOCK:]
        out_ref[b] = mixed.astype(BF16)


def finish_kernel(parts_ref, tokens_ref, out_ref):
    total = tokens_ref[...].astype(F32)
    for b in range(PARTS):
        total += parts_ref[b].astype(F32)
    out_ref[...] = total.astype(BF16)


def call(kernel, shape, *operands):
    return pl.pallas_call(
        kernel,
        out_shape=jax.ShapeDtypeStruct(shape, BF16),
        compiler_params=pltpu.CompilerParams(vmem_limit_bytes=VMEM),
    )(*operands)


def shift(x, axes, count, step):
    return lax.ppermute(x, axes, [(i, (i + step) % count) for i in range(count)])


def local(tokens, modulation, w_qkv, w_out, stale, text):
    w_heads = lax.all_gather(w_out, "guidance", axis=0, tiled=True)
    own = stale.reshape(2, BLOCK, 2 * HEAD)
    far = shift(own, "zf", 4, 2)
    features = lax.all_to_all(
        jnp.broadcast_to(tokens[None], (PARTS, BLOCK, COLS)), "tensor", 0, 0
    )
    pair = jnp.stack([own, far])
    pair, features = lax.optimization_barrier((pair, features))
    quad = shift(pair, "zf", 4, 1)
    up = shift(pair, ("zf", "zb"), 8, 1)
    down = shift(pair, ("zf", "zb"), 8, -1)
    ask = call(project_kernel, (2 * SHARE, ASK, HEAD), features, modulation, w_qkv)
    group = ("guidance", "za", "core")
    ask = lax.all_to_all(ask, group, 0, 0)
    text = text.reshape(2, -1, 2 * HEAD)
    reply = call(attend_kernel, (2 * SHARE, REPLY, HEAD), ask, pair, quad, up, down, text)
    reply = lax.all_to_all(reply, group, 0, 0)
    parts = call(output_kernel, (PARTS, BLOCK, COLS), reply, modulation, w_heads)
    parts = lax.all_to_all(parts, "tensor", 0, 0)
    return call(finish_kernel, (BLOCK, COLS), parts, tokens)


def solution(mesh):
    fine = jax.sharding.Mesh(
        mesh.devices.reshape(4, 2, 2, 2, 8, 2), ("zf", "zb", "za", "core", "tensor", "guidance")
    )
    patch = ("zf", "zb", "za", "core")
    in_specs = (
        P(patch, "tensor"),
        P(),
        P(None, None, ("tensor", "guidance")),
        P(("tensor", "guidance"), None),
        P(None, "guidance", patch, "tensor"),
        P(None, "guidance", None, "tensor"),
    )
    return jax.shard_map(
        local, mesh=fine, in_specs=in_specs, out_specs=P(patch, "tensor"), check_vma=False
    )
```

time: 309 us -> 172 us (0.56)
  waiting for transfers between devices: 226 us -> 75.1 us
  starting transfers between devices: 0.16 us -> 52.7 us
  local copies, waits for them, and re-layouts: 24.2 us -> 4.38 us
  matrix products: 11.1 us -> 0 us
  blocking collectives: 26.9 us -> 15.9 us
  Pallas kernels: 0 us -> 8.53 us
  other arithmetic: 6.32 us -> 0.93 us
    all_gather x3 -> x1, waiting for transfers between devices: 133 us -> 38.3 us  [local(): w_heads = lax.all_gather(w_out, 'guidance', axis=0, tiled=True)]
    psum x1 -> x0, waiting for transfers between devices: 48.9 us -> none  [local(): guided = lax.psum(partial_sum, 'guidance').astype(jnp.float32)]
    unnamed x6 -> x1, waiting for transfers between devices: 44.3 us -> 0.71 us
    ppermute x0 -> x4, waiting for transfers between devices: none -> 36.1 us  [shift(): lax.ppermute(x, axes, [(i, (i + step) % count) for i in range(count)])]
    all_gather x1 -> x0, blocking collectives: 26.9 us -> none  [local(): gathered = lax.all_gather(tokens, 'tensor', axis=1, tiled=True)]
    ppermute x0 -> x4, starting transfers between devices: none -> 26.9 us  [shift(): lax.ppermute(x, axes, [(i, (i + step) % count) for i in range(count)])]
    all_to_all x0 -> x3, starting transfers between devices: none -> 25.8 us  [the longest x1 14.8 us: local(): ask = lax.all_to_all(ask, group, 0, 0)]
    all_to_all x0 -> x1, blocking collectives: none -> 15.9 us  [local(): parts = lax.all_to_all(parts, 'tensor', 0, 0)]
  transfers between devices with their start and end apart: 5 -> 8, of which waited for: 5 -> 4; matrix products, arithmetic and copies ran while one was open for 11% -> 1% of each run, Pallas kernels for 0% -> 0%
where the time goes in v1:
time: 172 us; the launch traced here: 171 us
  waiting for transfers between devices  75.1 us (44%)
  starting transfers between devices  52.7 us (31%)
  blocking collectives  15.9 us (9%)
  between operations  13.5 us (8%)
  Pallas kernels  8.53 us (5%)
  local copies, waits for them, and re-layouts  4.38 us (3%)
    all_gather x1, waiting for transfers between devices, local(): w_heads = lax.all_gather(w_out, 'guidance', axis=0, tiled=True)  38.3 us
    ppermute x4, waiting for transfers between devices, shift(): lax.ppermute(x, axes, [(i, (i + step) % count) for i in range(count)])  36.1 us
    ppermute x4, starting transfers between devices, shift(): lax.ppermute(x, axes, [(i, (i + step) % count) for i in range(count)])  26.9 us
    all_to_all x1, blocking collectives, local(): parts = lax.all_to_all(parts, 'tensor', 0, 0)  15.9 us
    all_to_all x1, starting transfers between devices, local(): ask = lax.all_to_all(ask, group, 0, 0)  14.8 us
    pallas_call x4, Pallas kernels, call(): pl.pallas_call(kernel, out_shape=jax.ShapeDtypeStruct(shape, BF16), compi...  8.53 us
    all_to_all x1, starting transfers between devices, local(): lax.all_to_all(jnp.broadcast_to(tokens[None], (PARTS, BLOCK, COLS)), 'ten...  5.95 us
    all_to_all x1, starting transfers between devices, local(): reply = lax.all_to_all(reply, group, 0, 0)  5.02 us
  transfers between devices with their start and end apart: 8, of which 4 were waited for; matrix products, arithmetic and copies ran while one was open for 1% of the time, Pallas kernels for 0%

profile of v1, /device:TPU:1, one launch (start us, length us, event | category | flops | bytes accessed | tf_op | source)
XLA Modules:
  0.0 171.0 jit_solution(8567849153289361410)
XLA Ops:
  6.5 0.0 copy-start.5
  6.5 0.0 copy-start.3
  6.5 0.0 copy-start
  6.5 2.0 %broadcast_in_dim.2 = bf16[8,128,384]{2,1,0:T(8,128)(2,1)} broadcast(bf16[128,384]{1,0:T(8,128)(2,1)} %tokens_ref.1), dimensions={1,2} | broadcast | bytes 884736 | tf_op jit(solution)/shard_map/broadcast_in_dim | solution.py:177
  8.5 5.9 %all-to-all-start = ((bf16[8,128,384]{2,1,0:T(8,128)(2,1)}), bf16[8,128,384]{2,1,0:T(8,128)(2,1)S(1)}, u32[]{:S(2)}, u32[]{:S(2)}) async-start(bf16[8,128,384]{2,1,0:T(8,128)(2,1)} %broadcast_in_dim.2), calls=%async_computation | async-start | bytes 1572864 | tf_op jit(solution)/shard_map/all_to_all | solution.py:176
  14.5 0.0 copy-done.5
  14.5 15.4 %collective-permute-start = (bf16[2,128,256]{2,1,0:T(8,128)(2,1)S(1)}, bf16[2,128,256]{2,1,0:T(8,128)(2,1)S(1)}, u32[]{:S(2)}, u32[]{:S(2)}) collective-permute-start(bf16[2,128,256]{2,1,0:T(8,128)(2,1)S(1)} %bitcast.6), channel_id=1, source_target_pairs={{0,256},{128,384},{256,0},{384,128},{1,257},{129,385},{257,1},{385... | collective-permute-start | bytes 393224 | tf_op jit(solution)/shard_map/ppermute | solution.py:169
  29.9 2.6 %collective-permute-done = bf16[2,128,256]{2,1,0:T(8,128)(2,1)S(1)} collective-permute-done((bf16[2,128,256]{2,1,0:T(8,128)(2,1)S(1)}, bf16[2,128,256]{2,1,0:T(8,128)(2,1)S(1)}, u32[]{:S(2)}, u32[]{:S(2)}) %collective-permute-start) | collective-permute-done | bytes 131104 | tf_op jit(solution)/shard_map/ppermute | solution.py:169
  32.6 0.9 pad_maximum_fusion.kv0
  33.5 0.0 all-to-all-done.x_ref
  33.5 0.0 copy-done.3
  33.5 0.0 copy-done
  33.6 2.7 %shard_map.64 = bf16[8,192,128]{2,1,0:T(8,128)(2,1)} custom-call(bf16[8,128,384]{2,1,0:T(8,128)(2,1)S(1)} %all-to-all-done.x_ref, f32[3,2,3072]{2,1,0:T(2,128)S(1)} %copy-done.3, bf16[3,3072,128]{2,1,0:T(8,128)(2,1)S(1)} %copy-done), custom_call_target="tpu_custom_call" | custom-call | tf_op jit(solution)/shard_map/pallas_call | solution.py:161
  36.2 14.8 %all-to-all-start.1 = ((bf16[8,192,128]{2,1,0:T(8,128)(2,1)}), bf16[8,192,128]{2,1,0:T(8,128)(2,1)S(1)}, u32[]{:S(2)}, u32[]{:S(2)}) async-start(bf16[8,192,128]{2,1,0:T(8,128)(2,1)} %shard_map.64), calls=%async_computation.1 | async-start | bytes 786432 | tf_op jit(solution)/shard_map/all_to_all | solution.py:186
  51.1 3.4 %collective-permute-start.1 = (bf16[2,2,128,256]{3,2,1,0:T(8,128)(2,1)S(1)}, bf16[2,2,128,256]{3,2,1,0:T(8,128)(2,1)S(1)}, u32[]{:S(2)}, u32[]{:S(2)}) collective-permute-start(bf16[2,2,128,256]{3,2,1,0:T(8,128)(2,1)S(1)} %pad_maximum_fusion.kv0), channel_id=1, source_target_pairs={{0,128},{128,256},{256,384},{384,0},{1,129},{129,257},{257,385},{3... | collective-permute-start | bytes 786440 | tf_op jit(solution)/shard_map/ppermute | solution.py:169
  54.4 5.7 %collective-permute-start.2 = (bf16[2,2,128,256]{3,2,1,0:T(8,128)(2,1)S(1)}, bf16[2,2,128,256]{3,2,1,0:T(8,128)(2,1)S(1)}, u32[]{:S(2)}, u32[]{:S(2)}) collective-permute-start(bf16[2,2,128,256]{3,2,1,0:T(8,128)(2,1)S(1)} %pad_maximum_fusion.kv0), channel_id=1, source_target_pairs={{0,64},{64,128},{128,192},{192,256},{256,320},{320,384},{384,448},... | collective-permute-start | bytes 786440 | tf_op jit(solution)/shard_map/ppermute | solution.py:169
  60.1 2.4 %collective-permute-start.3 = (bf16[2,2,128,256]{3,2,1,0:T(8,128)(2,1)S(1)}, bf16[2,2,128,256]{3,2,1,0:T(8,128)(2,1)S(1)}, u32[]{:S(2)}, u32[]{:S(2)}) collective-permute-start(bf16[2,2,128,256]{3,2,1,0:T(8,128)(2,1)S(1)} %pad_maximum_fusion.kv0), channel_id=1, source_target_pairs={{0,448},{64,0},{128,64},{192,128},{256,192},{320,256},{384,320},{4... | collective-permute-start | bytes 786440 | tf_op jit(solution)/shard_map/ppermute | solution.py:169
  62.5 8.5 %collective-permute-done.1.kv1 = bf16[2,2,128,256]{3,2,1,0:T(8,128)(2,1)S(1)} collective-permute-done((bf16[2,2,128,256]{3,2,1,0:T(8,128)(2,1)S(1)}, bf16[2,2,128,256]{3,2,1,0:T(8,128)(2,1)S(1)}, u32[]{:S(2)}, u32[]{:S(2)}) %collective-permute-start.1) | collective-permute-done | bytes 262176 | tf_op jit(solution)/shard_map/ppermute | solution.py:169
  71.0 24.9 %collective-permute-done.2.kv2 = bf16[2,2,128,256]{3,2,1,0:T(8,128)(2,1)S(1)} collective-permute-done((bf16[2,2,128,256]{3,2,1,0:T(8,128)(2,1)S(1)}, bf16[2,2,128,256]{3,2,1,0:T(8,128)(2,1)S(1)}, u32[]{:S(2)}, u32[]{:S(2)}) %collective-permute-start.2) | collective-permute-done | bytes 262176 | tf_op jit(solution)/shard_map/ppermute | solution.py:169
  95.9 0.0 collective-permute-done.3.kv3
  95.9 0.0 all-to-all-done.1.ask_ref
  95.9 0.0 copy-start.4
  95.9 0.9 copy-done.4
  96.9 3.4 %shard_map.65 = bf16[8,272,128]{2,1,0:T(8,128)(2,1)} custom-call(bf16[8,192,128]{2,1,0:T(8,128)(2,1)S(1)} %all-to-all-done.1.ask_ref, bf16[2,2,128,256]{3,2,1,0:T(8,128)(2,1)S(1)} %pad_maximum_fusion.kv0, bf16[2,2,128,256]{3,2,1,0:T(8,128)(2,1)S(1)} %collective-permute-done.1.kv1, bf16[2,2,128,256]{3,2,1,0:T(8,128)(2,1)S(1)} %collective-permute-done.2.kv2, ...), custom_call_target="tpu_custom_call" | custom-call | tf_op jit(solution)/shard_map/pallas_call | solution.py:161
  100.3 5.0 %all-to-all-start.2 = ((bf16[8,272,128]{2,1,0:T(8,128)(2,1)}), bf16[8,272,128]{2,1,0:T(8,128)(2,1)S(1)}, u32[]{:S(2)}, u32[]{:S(2)}) async-start(bf16[8,272,128]{2,1,0:T(8,128)(2,1)} %shard_map.65), calls=%async_computation.2 | async-start | bytes 1114112 | tf_op jit(solution)/shard_map/all_to_all | solution.py:189
  105.3 0.0 all-gather.2.cloned.1.call-start
  105.3 0.0 copy-start.2
  105.3 0.7 all-gather.2.cloned.1.call-update
  106.0 38.3 %all-gather.2.cloned.1.call-done.w_ref = bf16[256,3072]{1,0:T(8,128)(2,1)} async-done(((bf16[128,3072]{1,0:T(8,128)(2,1)}), bf16[256,3072]{1,0:T(8,128)(2,1)}) %all-gather.2.cloned.1.call-update) | async-done | bytes 1572880 | tf_op jit(solution)/shard_map/all_gather | solution.py:173
  144.4 0.0 all-to-all-done.2.reply_ref
  144.4 0.0 copy-start.1
  144.4 1.4 copy-done.1
  145.8 1.7 shard_map.66
  147.5 15.9 %all_to_all.20.parts_ref = bf16[8,128,384]{2,1,0:T(8,128)(2,1)S(1)} all-to-all(bf16[8,128,384]{2,1,0:T(8,128)(2,1)S(1)} %shard_map.66), channel_id=1, replica_groups=mesh['zf'=4,'zb'=2,'za'=2,'core'=2,'tensor'=8,'guidance'=2] {'tensor'}, dimensions={0} | all-to-all | bytes 1572864 | tf_op jit(solution)/shard_map/all_to_all | solution.py:191
  163.4 0.0 copy-done.2
  163.4 0.8 shard_map.67
Async XLA Ops:
  6.5 8.0 %copy-start.5 = (bf16[2,1,128,256]{3,2,1,0:T(8,128)(2,1)S(1)}, bf16[2,1,128,256]{3,2,1,0:T(8,128)(2,1)}, u32[]{:S(2)}) copy-start(bf16[2,1,128,256]{3,2,1,0:T(8,128)(2,1)} %param.10) | copy-start | bytes 393220
  6.5 27.0 %copy-start.3 = (f32[3,2,3072]{2,1,0:T(2,128)S(1)}, f32[3,2,3072]{2,1,0:T(2,128)}, u32[]{:S(2)}) copy-start(f32[3,2,3072]{2,1,0:T(2,128)} %mod_ref.3) | copy-start | bytes 221188
  6.5 27.0 %copy-start = (bf16[3,3072,128]{2,1,0:T(8,128)(2,1)S(1)}, bf16[3,3072,128]{2,1,0:T(8,128)(2,1)}, u32[]{:S(2)}) copy-start(bf16[3,3072,128]{2,1,0:T(8,128)(2,1)} %w_ref.1) | copy-start | bytes 7077892
  8.5 25.0 %all-to-all-start = ((bf16[8,128,384]{2,1,0:T(8,128)(2,1)}), bf16[8,128,384]{2,1,0:T(8,128)(2,1)S(1)}, u32[]{:S(2)}, u32[]{:S(2)}) async-start(bf16[8,128,384]{2,1,0:T(8,128)(2,1)} %broadcast_in_dim.2), calls=%async_computation | async-start | bytes 1572864 | tf_op jit(solution)/shard_map/all_to_all | solution.py:176
  14.5 18.1 %collective-permute-start = (bf16[2,128,256]{2,1,0:T(8,128)(2,1)S(1)}, bf16[2,128,256]{2,1,0:T(8,128)(2,1)S(1)}, u32[]{:S(2)}, u32[]{:S(2)}) collective-permute-start(bf16[2,128,256]{2,1,0:T(8,128)(2,1)S(1)} %bitcast.6), channel_id=1, source_target_pairs={{0,256},{128,384},{256,0},{384,128},{1,257},{129,385},{257,1},{385... | collective-permute-start | bytes 393224 | tf_op jit(solution)/shard_map/ppermute | solution.py:169
  36.2 59.7 %all-to-all-start.1 = ((bf16[8,192,128]{2,1,0:T(8,128)(2,1)}), bf16[8,192,128]{2,1,0:T(8,128)(2,1)S(1)}, u32[]{:S(2)}, u32[]{:S(2)}) async-start(bf16[8,192,128]{2,1,0:T(8,128)(2,1)} %shard_map.64), calls=%async_computation.1 | async-start | bytes 786432 | tf_op jit(solution)/shard_map/all_to_all | solution.py:186
  51.1 20.0 %collective-permute-start.1 = (bf16[2,2,128,256]{3,2,1,0:T(8,128)(2,1)S(1)}, bf16[2,2,128,256]{3,2,1,0:T(8,128)(2,1)S(1)}, u32[]{:S(2)}, u32[]{:S(2)}) collective-permute-start(bf16[2,2,128,256]{3,2,1,0:T(8,128)(2,1)S(1)} %pad_maximum_fusion.kv0), channel_id=1, source_target_pairs={{0,128},{128,256},{256,384},{384,0},{1,129},{129,257},{257,385},{3... | collective-permute-start | bytes 786440 | tf_op jit(solution)/shard_map/ppermute | solution.py:169
  54.4 41.5 %collective-permute-start.2 = (bf16[2,2,128,256]{3,2,1,0:T(8,128)(2,1)S(1)}, bf16[2,2,128,256]{3,2,1,0:T(8,128)(2,1)S(1)}, u32[]{:S(2)}, u32[]{:S(2)}) collective-permute-start(bf16[2,2,128,256]{3,2,1,0:T(8,128)(2,1)S(1)} %pad_maximum_fusion.kv0), channel_id=1, source_target_pairs={{0,64},{64,128},{128,192},{192,256},{256,320},{320,384},{384,448},... | collective-permute-start | bytes 786440 | tf_op jit(solution)/shard_map/ppermute | solution.py:169
  60.1 35.8 %collective-permute-start.3 = (bf16[2,2,128,256]{3,2,1,0:T(8,128)(2,1)S(1)}, bf16[2,2,128,256]{3,2,1,0:T(8,128)(2,1)S(1)}, u32[]{:S(2)}, u32[]{:S(2)}) collective-permute-start(bf16[2,2,128,256]{3,2,1,0:T(8,128)(2,1)S(1)} %pad_maximum_fusion.kv0), channel_id=1, source_target_pairs={{0,448},{64,0},{128,64},{192,128},{256,192},{320,256},{384,320},{4... | collective-permute-start | bytes 786440 | tf_op jit(solution)/shard_map/ppermute | solution.py:169
  95.9 1.0 copy-start.4
  100.3 44.1 %all-to-all-start.2 = ((bf16[8,272,128]{2,1,0:T(8,128)(2,1)}), bf16[8,272,128]{2,1,0:T(8,128)(2,1)S(1)}, u32[]{:S(2)}, u32[]{:S(2)}) async-start(bf16[8,272,128]{2,1,0:T(8,128)(2,1)} %shard_map.65), calls=%async_computation.2 | async-start | bytes 1114112 | tf_op jit(solution)/shard_map/all_to_all | solution.py:189
  105.3 39.1 %all-gather.2.cloned.1.call-start = ((), (), s32[]{:S(2)}) async-start(), calls=%async_computation.4 | async-start | bytes 2359296 | tf_op jit(solution)/shard_map/all_gather | solution.py:173
  105.3 58.1 %copy-start.2 = (bf16[128,384]{1,0:T(8,128)(2,1)S(1)}, bf16[128,384]{1,0:T(8,128)(2,1)}, u32[]{:S(2)}) copy-start(bf16[128,384]{1,0:T(8,128)(2,1)} %tokens_ref.1) | copy-start | bytes 294916
  144.4 1.4 copy-start.1
Sparse Core Ops, SparseCore 0:
  108.2 36.1 all-gather.1

commit v2 on v1

--- a/solution.py
+++ b/solution.py
@@ -15,7 +15,7 @@
 BLOCK = 128
 PARTS = 8
 COLS = 384
-SHARE = 4
+SHARE = 2
 FRESH = BLOCK // SHARE
 ASK = BLOCK + 2 * FRESH
 REPLY = 2 * BLOCK + 16
@@ -67,14 +67,15 @@
             out_ref[d, BLOCK + FRESH : ASK, :] = value[rows]
 
 
-def attend_kernel(ask_ref, kv0, kv1, kv2, kv3, text_ref, out_ref):
-    own = lax.axis_index("za") * 2 + lax.axis_index("core")
+def attend_kernel(ask_ref, kv_ref, text_ref, out_ref):
+    own = lax.axis_index("za")
+    block = lax.axis_index("zf") * 4 + lax.axis_index("zb") * 2 + lax.axis_index("core")
     text_rows = text_ref.shape[1] // SHARE
     first = pl.multiple_of(own * text_rows, text_rows)
     query_rows = SHARE * BLOCK
     row_block = lax.broadcasted_iota(jnp.int32, (query_rows, 1), 0) // BLOCK
     col = lax.broadcasted_iota(jnp.int32, (1, 2 * BLOCK), 1)
-    own_stale = (row_block == own) & (col < BLOCK)
+    own_block = jnp.where(row_block == own, block, -1)
     other_fresh = row_block != col[:, :BLOCK] // FRESH
     lane = lax.broadcasted_iota(jnp.int32, (1, HEAD), 1)
     stats = jnp.zeros((BLOCK, HEAD), F32)
@@ -83,12 +84,10 @@
         mine = slice(h * SHARE, (h + 1) * SHARE)
         query = ask_ref[mine, 0:BLOCK, :].reshape(query_rows, HEAD)
         scores, values = [], []
-        for n, kv in enumerate((kv0, kv1, kv2, kv3)):
-            s = nt(query, kv[:, 0, :, cols].reshape(2 * BLOCK, HEAD))
-            if n == 0:
-                s = jnp.where(own_stale, NEGATIVE, s)
-            scores.append(s)
-            values.append(kv[:, 1, :, cols].reshape(2 * BLOCK, HEAD))
+        for n in range(0, kv_ref.shape[0], 2):
+            s = nt(query, kv_ref[n : n + 2, 0, :, cols].reshape(2 * BLOCK, HEAD))
+            scores.append(jnp.where(own_block == col // BLOCK + n, NEGATIVE, s))
+            values.append(kv_ref[n : n + 2, 1, :, cols].reshape(2 * BLOCK, HEAD))
         s = nt(query, ask_ref[mine, BLOCK : BLOCK + FRESH, :].reshape(BLOCK, HEAD))
         scores.append(jnp.where(other_fresh, NEGATIVE, s))
         values.append(ask_ref[mine, BLOCK + FRESH : ASK, :].reshape(BLOCK, HEAD))
@@ -121,9 +120,11 @@
             out_ref[g * SHARE + b, 2 * BLOCK : REPLY, :] = stats[16 * b : 16 * b + 16]
 
 
-def output_kernel(reply_ref, mod_ref, w_ref, out_ref):
-    stats = jnp.concatenate([reply_ref[s, 2 * BLOCK : REPLY, :].astype(F32) for s in range(2 * SHARE)], axis=0)
-    stats = jnp.transpose(stats)
+def output_kernel(reply_ref, mod_ref, w_ref, other_ref, out_ref):
+    flip = lax.axis_index("guidance") == 1
+    stats = [reply_ref[s, 2 * BLOCK : REPLY, :].astype(F32) for s in range(2 * SHARE)]
+    stats.append(jnp.zeros((HEAD - 32 * SHARE, HEAD), F32))
+    stats = jnp.transpose(jnp.concatenate(stats, axis=0))
     attended = []
     for p in range(2):
         heads = []
@@ -132,19 +133,22 @@
             for j in range(SHARE):
                 c = 16 * (p * SHARE + j) + 3 * h
                 levels.append(stats[:, c : c + 1] + stats[:, c + 1 : c + 2] + stats[:, c + 2 : c + 3])
-            top = jnp.maximum(jnp.maximum(levels[0], levels[1]), jnp.maximum(levels[2], levels[3]))
+            top = jnp.maximum(levels[0], levels[1])
             shares = [jnp.exp2(level - top) for level in levels]
-            total = shares[0] + shares[1] + shares[2] + shares[3]
+            total = shares[0] + shares[1]
             summed = jnp.zeros((BLOCK, HEAD), F32)
             for j in range(SHARE):
                 part = reply_ref[p * SHARE + j, h * BLOCK : (h + 1) * BLOCK, :].astype(F32)
                 summed += shares[j] * part
-            heads.append((summed / total).astype(BF16))
-        attended.append(jnp.concatenate(heads, axis=1))
-    attended = jnp.concatenate(attended, axis=0)
+            heads.append(summed / total)
+        attended.append(heads)
+    own = [jnp.where(flip, heads[1], heads[0]).astype(BF16) for heads in attended]
+    other = [jnp.where(flip, heads[0], heads[1]).astype(BF16) for heads in attended]
+    attended = jnp.concatenate([jnp.concatenate(own, axis=0), jnp.concatenate(other, axis=0)], axis=1)
     for b in range(PARTS):
         cols = slice(b * COLS, (b + 1) * COLS)
-        branch = nn(attended, w_ref[:, cols])
+        weights = jnp.concatenate([w_ref[:, cols], other_ref[:, cols]], axis=0)
+        branch = nn(attended, weights)
         mixed = (GUIDE * mod_ref[2, 0:1, cols]) * branch[:BLOCK]
         mixed += ((1.0 - GUIDE) * mod_ref[2, 1:2, cols]) * branch[BLOCK:]
         out_ref[b] = mixed.astype(BF16)
@@ -165,29 +169,34 @@
     )(*operands)
 
 
-def shift(x, axes, count, step):
-    return lax.ppermute(x, axes, [(i, (i + step) % count) for i in range(count)])
+def together(run, *operands):
+    shapes = jax.eval_shape(run, *operands)
+    return lax.cond(
+        lax.axis_index("za") < 2,
+        run,
+        lambda *_: jax.tree.map(lambda s: jnp.zeros(s.shape, s.dtype), shapes),
+        *operands,
+    )
 
 
 def local(tokens, modulation, w_qkv, w_out, stale, text):
-    w_heads = lax.all_gather(w_out, "guidance", axis=0, tiled=True)
-    own = stale.reshape(2, BLOCK, 2 * HEAD)
-    far = shift(own, "zf", 4, 2)
-    features = lax.all_to_all(
-        jnp.broadcast_to(tokens[None], (PARTS, BLOCK, COLS)), "tensor", 0, 0
-    )
-    pair = jnp.stack([own, far])
-    pair, features = lax.optimization_barrier((pair, features))
-    quad = shift(pair, "zf", 4, 1)
-    up = shift(pair, ("zf", "zb"), 8, 1)
-    down = shift(pair, ("zf", "zb"), 8, -1)
-    ask = call(project_kernel, (2 * SHARE, ASK, HEAD), features, modulation, w_qkv)
-    group = ("guidance", "za", "core")
-    ask = lax.all_to_all(ask, group, 0, 0)
+    group = ("guidance", "za")
+    stale = lax.all_gather(stale.reshape(2, BLOCK, 2 * HEAD), ("zf", "zb", "core"))
+
+    def ask(tokens, modulation, w_qkv, w_out):
+        features = lax.all_to_all(
+            jnp.broadcast_to(tokens[None], (PARTS, BLOCK, COLS)), "tensor", 0, 0
+        )
+        message = call(project_kernel, (2 * SHARE, ASK, HEAD), features, modulation, w_qkv)
+        message = lax.all_to_all(message, group, 0, 0)
+        message, w_out = lax.optimization_barrier((message, w_out))
+        return message, lax.ppermute(w_out, "guidance", [(0, 1), (1, 0)])
+
+    message, other_w = together(ask, tokens, modulation, w_qkv, w_out)
     text = text.reshape(2, -1, 2 * HEAD)
-    reply = call(attend_kernel, (2 * SHARE, REPLY, HEAD), ask, pair, quad, up, down, text)
-    reply = lax.all_to_all(reply, group, 0, 0)
-    parts = call(output_kernel, (PARTS, BLOCK, COLS), reply, modulation, w_heads)
+    message = call(attend_kernel, (2 * SHARE, REPLY, HEAD), message, stale, text)
+    message = lax.all_to_all(message, group, 0, 0)
+    parts = call(output_kernel, (PARTS, BLOCK, COLS), message, modulation, w_out, other_w)
     parts = lax.all_to_all(parts, "tensor", 0, 0)
     return call(finish_kernel, (BLOCK, COLS), parts, tokens)
 

time: 172 us -> 110 us (0.64)
  starting transfers between devices: 52.7 us -> 2.94 us
  waiting for transfers between devices: 75.1 us -> 27.7 us
  blocking collectives: 15.9 us -> 54.9 us
    all_to_all x0 -> x3, blocking collectives: none -> 40.6 us  [the longest x1 15.1 us: ask(): lax.all_to_all(jnp.broadcast_to(tokens[None], (PARTS, BLOCK, COLS)), 'ten...]
    all_gather x1, waiting for transfers between devices: 38.3 us -> 12 us  [local(): lax.all_gather(stale.reshape(2, BLOCK, 2 * HEAD), ('zf', 'zb', 'core'))]
    all_to_all x3 -> x0, starting transfers between devices: 25.8 us -> none  [the longest x1 14.8 us: local(): ask = lax.all_to_all(ask, group, 0, 0)]
    ppermute x4 -> x1, starting transfers between devices: 26.9 us -> 2.93 us  [ask(): return (message, lax.ppermute(w_out, 'guidance', [(0, 1), (1, 0)]))]
    ppermute x4 -> x1, waiting for transfers between devices: 36.1 us -> 15 us  [ask(): return (message, lax.ppermute(w_out, 'guidance', [(0, 1), (1, 0)]))]
  transfers between devices with their start and end apart: 8 -> 2, of which waited for: 4 -> 2; matrix products, arithmetic and copies ran while one was open for 1% -> 1% of each run, Pallas kernels for 0% -> 2%
where the time goes in v2:
time: 110 us; the launch traced here: 109 us
  blocking collectives  54.9 us (50%)
  waiting for transfers between devices  27.7 us (25%)
  between operations  13.4 us (12%)
  Pallas kernels  7.31 us (7%)
  starting transfers between devices  2.94 us (3%)
  local copies, waits for them, and re-layouts  2.73 us (2%)
    all_to_all x1, blocking collectives, ask(): lax.all_to_all(jnp.broadcast_to(tokens[None], (PARTS, BLOCK, COLS)), 'ten...  15.1 us
    ppermute x1, waiting for transfers between devices, ask(): return (message, lax.ppermute(w_out, 'guidance', [(0, 1), (1, 0)]))  15 us
    all_to_all x1, blocking collectives, local(): parts = lax.all_to_all(parts, 'tensor', 0, 0)  14.3 us
    all_to_all x1, blocking collectives, ask(): message = lax.all_to_all(message, group, 0, 0)  14 us
    all_gather x1, waiting for transfers between devices, local(): lax.all_gather(stale.reshape(2, BLOCK, 2 * HEAD), ('zf', 'zb', 'core'))  12 us
    all_to_all x1, blocking collectives, local(): message = lax.all_to_all(message, group, 0, 0)  11.5 us
    pallas_call x4, Pallas kernels, call(): pl.pallas_call(kernel, out_shape=jax.ShapeDtypeStruct(shape, BF16), compi...  7.31 us
    ppermute x1, starting transfers between devices, ask(): return (message, lax.ppermute(w_out, 'guidance', [(0, 1), (1, 0)]))  2.93 us
  transfers between devices with their start and end apart: 2, of which 2 were waited for; matrix products, arithmetic and copies ran while one was open for 1% of the time, Pallas kernels for 2%

profile of v2, /device:TPU:1, one launch (start us, length us, event | category | flops | bytes accessed | tf_op | source)
XLA Modules:
  0.0 109.1 jit_solution(11993710338858301402)
XLA Ops:
  6.5 0.0 all-gather.3.cloned.1.call-start
  6.5 0.7 all-gather.3.cloned.1.call-update
  7.3 0.0 copy-start.1
  7.3 50.1 %conditional.1 = (bf16[4,256,128]{2,1,0:T(8,128)(2,1)S(1)}, bf16[128,3072]{1,0:T(8,128)(2,1)}) conditional(s32[]{:T(128)} %convert_element_type.3, () %tuple.14, (bf16[128,384]{1,0:T(8,128)(2,1)}, f32[3,2,3072]{2,1,0:T(2,128)}, bf16[3,3072,128]{2,1,0:T(8,128)(2,1)}, bf16[128,3072]{1,0:T(8,128)(2,1)}) %tuple.15), branch_computations={%region_0.0_spmd, %region_1.0_spmd} | conditional | bytes 19005580 | solution.py:174
  7.3 0.0 copy-start.2
  7.3 0.0 copy-start.7
  7.3 1.1 %broadcast_in_dim.0 = bf16[8,128,384]{2,1,0:T(8,128)(2,1)S(1)} broadcast(bf16[128,384]{1,0:T(8,128)(2,1)} %get-tuple-element.13), dimensions={1,2} | broadcast | bytes 884736 | tf_op jit(solution)/shard_map/cond/branch_1_fun/broadcast_in_dim | solution.py:188
  8.4 15.1 %all_to_all.18.x_ref = bf16[8,128,384]{2,1,0:T(8,128)(2,1)S(1)} all-to-all(bf16[8,128,384]{2,1,0:T(8,128)(2,1)S(1)} %broadcast_in_dim.0), channel_id=1, replica_groups=mesh['zf'=4,'zb'=2,'za'=2,'core'=2,'tensor'=8,'guidance'=2] {'tensor'}, dimensions={0} | all-to-all | bytes 1572864 | tf_op jit(solution)/shard_map/cond/branch_1_fun/all_to_all | solution.py:187
  23.5 0.0 copy-start.4
  23.5 0.0 copy-done.2
  23.5 0.0 copy-done.7
  23.5 1.9 %branch_1_fun.1 = bf16[4,256,128]{2,1,0:T(8,128)(2,1)S(1)} custom-call(bf16[8,128,384]{2,1,0:T(8,128)(2,1)S(1)} %all_to_all.18.x_ref, f32[3,2,3072]{2,1,0:T(2,128)S(1)} %copy-done.7, bf16[3,3072,128]{2,1,0:T(8,128)(2,1)S(1)} %copy-done.2), custom_call_target="tpu_custom_call" | custom-call | tf_op jit(solution)/shard_map/cond/branch_1_fun/pallas_call | solution.py:165
  25.4 14.0 %all_to_all.19 = bf16[4,256,128]{2,1,0:T(8,128)(2,1)S(1)} all-to-all(bf16[4,256,128]{2,1,0:T(8,128)(2,1)S(1)} %branch_1_fun.1), channel_id=1, replica_groups=mesh['zf'=4,'zb'=2,'za'=2,'core'=2,'tensor'=8,'guidance'=2] {'guidance',..., dimensions={0} | all-to-all | bytes 524288 | tf_op jit(solution)/shard_map/cond/branch_1_fun/all_to_all | solution.py:191
  39.4 0.0 copy-done.4
  39.4 2.9 %collective-permute-start = (bf16[128,3072]{1,0:T(8,128)(2,1)S(1)}, bf16[128,3072]{1,0:T(8,128)(2,1)}, u32[]{:S(2)}, u32[]{:S(2)}) collective-permute-start(bf16[128,3072]{1,0:T(8,128)(2,1)S(1)} %copy-done.4), channel_id=1, source_target_pairs={{0,1},{1,0},{2,3},{3,2},{4,5},{5,4},{6,7},{7,6},{8,9},{9,8},{10,11... | collective-permute-start | bytes 2359304 | tf_op jit(solution)/shard_map/cond/branch_1_fun/ppermute | solution.py:193
  42.3 15.0 %collective-permute-done = bf16[128,3072]{1,0:T(8,128)(2,1)} collective-permute-done((bf16[128,3072]{1,0:T(8,128)(2,1)S(1)}, bf16[128,3072]{1,0:T(8,128)(2,1)}, u32[]{:S(2)}, u32[]{:S(2)}) %collective-permute-start) | collective-permute-done | bytes 786464 | tf_op jit(solution)/shard_map/cond/branch_1_fun/ppermute | solution.py:193
  57.4 12.0 %all-gather.3.cloned.1.call-done = bf16[32,1,128,256]{3,2,1,0:T(8,128)(2,1)} async-done(((bf16[2,1,128,256]{3,2,1,0:T(8,128)(2,1)}), bf16[32,1,128,256]{3,2,1,0:T(8,128)(2,1)}) %all-gather.3.cloned.1.call-update) | async-done | bytes 2097168 | tf_op jit(solution)/shard_map/all_gather | solution.py:184
  69.3 0.0 copy-done.1
  69.3 0.0 copy-start
  69.3 1.6 %copy-done = bf16[32,1,128,256]{3,2,1,0:T(8,128)(2,1)S(1)} copy-done((bf16[32,1,128,256]{3,2,1,0:T(8,128)(2,1)S(1)}, bf16[32,1,128,256]{3,2,1,0:T(8,128)(2,1)}, u32[]{:S(2)}) %copy-start) | copy-done | bytes 2097176
  70.9 0.0 copy-start.3
  70.9 0.0 copy-start.6
  70.9 2.2 %shard_map.65 = bf16[4,272,128]{2,1,0:T(8,128)(2,1)S(1)} custom-call(bf16[4,256,128]{2,1,0:T(8,128)(2,1)S(1)} %get-tuple-element.21.ask_ref, bf16[16,2,128,256]{3,2,1,0:T(8,128)(2,1)S(1)} %bitcast.2, bf16[2,256,256]{2,1,0:T(8,128)(2,1)S(1)} %bitcast.3), custom_call_target="tpu_custom_call" | custom-call | tf_op jit(solution)/shard_map/pallas_call | solution.py:165
  73.2 0.0 copy-start.5
  73.2 11.5 %all_to_all.20.reply_ref = bf16[4,272,128]{2,1,0:T(8,128)(2,1)S(1)} all-to-all(bf16[4,272,128]{2,1,0:T(8,128)(2,1)S(1)} %shard_map.65), channel_id=1, replica_groups=mesh['zf'=4,'zb'=2,'za'=2,'core'=2,'tensor'=8,'guidance'=2] {'guidance',..., dimensions={0} | all-to-all | bytes 557056 | tf_op jit(solution)/shard_map/all_to_all | solution.py:198
  84.7 0.0 copy-done.3
  84.7 0.0 copy-done.6
  84.7 2.4 %shard_map.66 = bf16[8,128,384]{2,1,0:T(8,128)(2,1)S(1)} custom-call(bf16[4,272,128]{2,1,0:T(8,128)(2,1)S(1)} %all_to_all.20.reply_ref, f32[3,2,3072]{2,1,0:T(2,128)S(1)} %copy-done.6, bf16[128,3072]{1,0:T(8,128)(2,1)S(1)} %copy-done.3, bf16[128,3072]{1,0:T(8,128)(2,1)} %get-tuple-element.22.other_ref), custom_call_target="tpu_custom_call" | custom-call | tf_op jit(solution)/shard_map/pallas_call | solution.py:165
  87.1 14.3 %all_to_all.21.parts_ref = bf16[8,128,384]{2,1,0:T(8,128)(2,1)S(1)} all-to-all(bf16[8,128,384]{2,1,0:T(8,128)(2,1)S(1)} %shard_map.66), channel_id=1, replica_groups=mesh['zf'=4,'zb'=2,'za'=2,'core'=2,'tensor'=8,'guidance'=2] {'tensor'}, dimensions={0} | all-to-all | bytes 1572864 | tf_op jit(solution)/shard_map/all_to_all | solution.py:200
  101.4 0.0 copy-done.5
  101.5 0.8 shard_map.67
Async XLA Ops:
  6.5 62.8 %all-gather.3.cloned.1.call-start = ((), (), s32[]{:S(2)}) async-start(), calls=%async_computation.4 | async-start | bytes 2228224 | tf_op jit(solution)/shard_map/all_gather | solution.py:184
  7.3 62.1 %copy-start.1 = (bf16[2,1,256,256]{3,2,1,0:T(8,128)(2,1)S(1)}, bf16[2,1,256,256]{3,2,1,0:T(8,128)(2,1)}, u32[]{:S(2)}) copy-start(bf16[2,1,256,256]{3,2,1,0:T(8,128)(2,1)} %param.13) | copy-start | bytes 786436
  7.3 16.3 %copy-start.2 = (bf16[3,3072,128]{2,1,0:T(8,128)(2,1)S(1)}, bf16[3,3072,128]{2,1,0:T(8,128)(2,1)}, u32[]{:S(2)}) copy-start(bf16[3,3072,128]{2,1,0:T(8,128)(2,1)} %get-tuple-element.24.w_ref) | copy-start | bytes 7077892 | tf_op jit(solution)/shard_map/cond
  7.3 16.3 %copy-start.7 = (f32[3,2,3072]{2,1,0:T(2,128)S(1)}, f32[3,2,3072]{2,1,0:T(2,128)}, u32[]{:S(2)}) copy-start(f32[3,2,3072]{2,1,0:T(2,128)} %get-tuple-element.14.mod_ref) | copy-start | bytes 221188 | tf_op jit(solution)/shard_map/cond
  23.5 15.9 %copy-start.4 = (bf16[128,3072]{1,0:T(8,128)(2,1)S(1)}, bf16[128,3072]{1,0:T(8,128)(2,1)}, u32[]{:S(2)}) copy-start(bf16[128,3072]{1,0:T(8,128)(2,1)} %get-tuple-element.18) | copy-start | bytes 2359300 | tf_op jit(solution)/shard_map/cond
  39.4 17.9 %collective-permute-start = (bf16[128,3072]{1,0:T(8,128)(2,1)S(1)}, bf16[128,3072]{1,0:T(8,128)(2,1)}, u32[]{:S(2)}, u32[]{:S(2)}) collective-permute-start(bf16[128,3072]{1,0:T(8,128)(2,1)S(1)} %copy-done.4), channel_id=1, source_target_pairs={{0,1},{1,0},{2,3},{3,2},{4,5},{5,4},{6,7},{7,6},{8,9},{9,8},{10,11... | collective-permute-start | bytes 2359304 | tf_op jit(solution)/shard_map/cond/branch_1_fun/ppermute | solution.py:193
  69.3 1.6 %copy-start = (bf16[32,1,128,256]{3,2,1,0:T(8,128)(2,1)S(1)}, bf16[32,1,128,256]{3,2,1,0:T(8,128)(2,1)}, u32[]{:S(2)}) copy-start(bf16[32,1,128,256]{3,2,1,0:T(8,128)(2,1)} %all-gather.3.cloned.1.call-done) | copy-start | bytes 6291460
  70.9 13.8 %copy-start.3 = (bf16[128,3072]{1,0:T(8,128)(2,1)S(1)}, bf16[128,3072]{1,0:T(8,128)(2,1)}, u32[]{:S(2)}) copy-start(bf16[128,3072]{1,0:T(8,128)(2,1)} %w_ref.1) | copy-start | bytes 2359300
  70.9 13.8 %copy-start.6 = (f32[3,2,3072]{2,1,0:T(2,128)S(1)}, f32[3,2,3072]{2,1,0:T(2,128)}, u32[]{:S(2)}) copy-start(f32[3,2,3072]{2,1,0:T(2,128)} %mod_ref.1) | copy-start | bytes 221188
  73.2 28.3 %copy-start.5 = (bf16[128,384]{1,0:T(8,128)(2,1)S(1)}, bf16[128,384]{1,0:T(8,128)(2,1)}, u32[]{:S(2)}) copy-start(bf16[128,384]{1,0:T(8,128)(2,1)} %tokens_ref.1) | copy-start | bytes 294916
Sparse Core Ops, SparseCore 0:
  9.5 59.7 all-gather.2

commit v3 on v1

v3 whole, which is shorter than its diff:
```python
import math

import jax
import jax.numpy as jnp
from jax import lax
from jax.experimental import pallas as pl
from jax.experimental.pallas import tpu as pltpu
from jax.sharding import PartitionSpec as P

HEAD = 128
GUIDE = 3.0
EPSILON = 1e-06
NEGATIVE = -1e30
BASE = math.log2(math.e) / math.sqrt(HEAD)
BLOCK = 128
PARTS = 8
COLS = 384
SHARE = 4
CHIPS = 2
QUERIES = SHARE * BLOCK
LEAF = BLOCK + 16
REPLY = 2 * BLOCK + 16
BF16 = jnp.bfloat16
F32 = jnp.float32
VMEM = 24 * 1024 * 1024


def nt(a, b):
    return lax.dot_general(a, b, (((1,), (1,)), ((), ())), preferred_element_type=F32)


def nn(a, b):
    return jnp.dot(a, b, preferred_element_type=F32)


def project_kernel(x_ref, mod_ref, w_ref, own_ref, away_ref):
    total = jnp.zeros((BLOCK, 1), F32)
    for b in range(PARTS):
        total += jnp.sum(x_ref[b].astype(F32), axis=-1, keepdims=True)
    average = total * (1.0 / (PARTS * COLS))
    total = jnp.zeros((BLOCK, 1), F32)
    for b in range(PARTS):
        centered = x_ref[b].astype(F32) - average
        total += jnp.sum(centered * centered, axis=-1, keepdims=True)
    inverse = lax.rsqrt(total * (1.0 / (PARTS * COLS)) + EPSILON)
    sums = [jnp.zeros((2 * BLOCK, HEAD), F32) for _ in range(3)]
    for b in range(PARTS):
        cols = slice(b * COLS, (b + 1) * COLS)
        normed = (x_ref[b].astype(F32) - average) * inverse
        both = [
            (normed * (1.0 + mod_ref[1, p : p + 1, cols]) + mod_ref[0, p : p + 1, cols]).astype(BF16)
            for p in range(2)
        ]
        both = jnp.concatenate(both, axis=0)
        for i in range(3):
            sums[i] += nn(both, w_ref[i, cols, :])

    def head_norm(v, scale):
        inverse = lax.rsqrt(jnp.mean(v * v, axis=-1, keepdims=True) + EPSILON) * scale
        return (v * inverse).astype(BF16)

    heads = head_norm(sums[0], BASE), head_norm(sums[1], 1.0), sums[2].astype(BF16)
    guidance = lax.axis_index("guidance")
    for p in range(2):
        rows = slice(p * BLOCK, (p + 1) * BLOCK)

        @pl.when(guidance == p)
        def _():
            for i in range(3):
                own_ref[i] = heads[i][rows]

        @pl.when(guidance != p)
        def _():
            for i in range(3):
                away_ref[i] = heads[i][rows]


def split_level(level):
    high = level.astype(BF16).astype(F32)
    middle = (level - high).astype(BF16).astype(F32)
    return high, middle, level - high - middle


def read_levels(stats):
    count = sum(s.shape[0] for s in stats) // 16
    stats = [s.astype(F32) for s in stats] + [jnp.zeros((HEAD - 16 * count, HEAD), F32)]
    stats = jnp.transpose(jnp.concatenate(stats, axis=0))
    return [
        [sum(stats[:, 16 * j + 3 * h + i : 16 * j + 3 * h + i + 1] for i in range(3)) for h in range(2)]
        for j in range(count)
    ]


def join(levels, parts):
    top = jnp.maximum(levels[0], levels[1])
    shares = [jnp.exp2(level - top) for level in levels]
    total = shares[0] + shares[1]
    joined = shares[0] * parts[0].astype(F32) + shares[1] * parts[1].astype(F32)
    return joined / total, top + jnp.log2(total)


def attend_kernel(query_ref, fresh_ref, kv0, kv1, kv2, kv3, kv4, text_ref, out_ref):
    own = lax.axis_index("za") * 2 + lax.axis_index("core")
    text_rows = text_ref.shape[1] // SHARE
    first = pl.multiple_of(own * text_rows, text_rows)
    row_block = lax.broadcasted_iota(jnp.int32, (QUERIES, 1), 0) // BLOCK
    col = lax.broadcasted_iota(jnp.int32, (1, 2 * BLOCK), 1)
    own_stale = (row_block == own) & (col < BLOCK)
    other_rows = row_block != own
    lane = lax.broadcasted_iota(jnp.int32, (1, HEAD), 1)
    stats = jnp.zeros((BLOCK, HEAD), F32)
    for h in range(2):
        cols = slice(h * HEAD, (h + 1) * HEAD)
        query = query_ref[:, h].reshape(QUERIES, HEAD)
        scores, values = [], []
        for n, kv in enumerate((kv0, kv1, kv2)):
            s = nt(query, kv[:, 0, :, cols].reshape(2 * BLOCK, HEAD))
            if n == 0:
                s = jnp.where(own_stale, NEGATIVE, s)
            scores.append(s)
            values.append(kv[:, 1, :, cols].reshape(2 * BLOCK, HEAD))
        for kv in (kv3, kv4):
            scores.append(nt(query, kv[0, :, cols]))
            values.append(kv[1, :, cols])
        scores.append(jnp.where(other_rows, NEGATIVE, nt(query, fresh_ref[h, 1])))
        values.append(fresh_ref[h, 2])
        scores.append(nt(query, text_ref[0, pl.ds(first, text_rows), cols]))
        values.append(text_ref[1, pl.ds(first, text_rows), cols])
        top = jnp.max(scores[0], axis=-1, keepdims=True)
        for s in scores[1:]:
            top = jnp.maximum(top, jnp.max(s, axis=-1, keepdims=True))
        total = jnp.zeros((QUERIES, 1), F32)
        summed = jnp.zeros((QUERIES, HEAD), F32)
        for s, v in zip(scores, values):
            weights = jnp.exp2(s - top)
            total += jnp.sum(weights, axis=-1, keepdims=True)
            summed += nn(weights.astype(BF16), v)
        summed = (summed / total).astype(BF16)
        pieces = split_level(top + jnp.log2(total))
        for b in range(SHARE):
            rows = slice(b * BLOCK, (b + 1) * BLOCK)
            out_ref[b, h * BLOCK : (h + 1) * BLOCK, :] = summed[rows]
            for i, piece in enumerate(pieces):
                stats = jnp.where(lane == 16 * b + 3 * h + i, piece[rows], stats)
    stats = jnp.transpose(stats).astype(BF16)
    for b in range(SHARE):
        out_ref[b, 2 * BLOCK : REPLY, :] = stats[16 * b : 16 * b + 16]


def join_kernel(mine_ref, cores_ref, out_ref):
    core = lax.axis_index("core")
    lane = lax.broadcasted_iota(jnp.int32, (1, HEAD), 1)
    stats = jnp.zeros((BLOCK, HEAD), F32)
    mine = [mine_ref[pl.ds(2 * b + core, 1)][0] for b in range(CHIPS)]
    other = [cores_ref[pl.ds(1 - core, 1), b][0] for b in range(CHIPS)]
    levels = read_levels([m[2 * BLOCK : REPLY] for m in mine + other])
    for b in range(CHIPS):
        for h in range(2):
            rows = slice(h * BLOCK, (h + 1) * BLOCK)
            joined, level = join(
                [levels[b][h], levels[CHIPS + b][h]], [mine[b][rows], other[b][rows]]
            )
            out_ref[h * CHIPS + b, 0:BLOCK, :] = joined.astype(BF16)
            for i, piece in enumerate(split_level(level)):
                stats = jnp.where(lane == 16 * (h * CHIPS + b) + i, piece, stats)
    stats = jnp.transpose(stats).astype(BF16)
    for d in range(2 * CHIPS):
        out_ref[d, BLOCK:LEAF, :] = stats[16 * d : 16 * d + 16]


def output_kernel(reply_ref, mod_ref, w_ref, out_ref):
    levels = read_levels([reply_ref[s, BLOCK:LEAF, :] for s in range(2 * CHIPS)])
    attended = []
    for p in range(2):
        pair = (p * CHIPS, p * CHIPS + 1)
        joined, _ = join([levels[s][0] for s in pair], [reply_ref[s, 0:BLOCK, :] for s in pair])
        attended.append(joined.astype(BF16))
    attended = jnp.concatenate(attended, axis=0)
    for b in range(PARTS):
        cols = slice(b * COLS, (b + 1) * COLS)
        branch = nn(attended, w_ref[:, cols])
        mixed = (GUIDE * mod_ref[2, 0:1, cols]) * branch[:BLOCK]
        mixed += ((1.0 - GUIDE) * mod_ref[2, 1:2, cols]) * branch[BLOCK:]
        out_ref[b] = mixed.astype(BF16)


def sum_kernel(parts_ref, out_ref):
    total = jnp.zeros(out_ref.shape, F32)
    for b in range(PARTS):
        total += parts_ref[b].astype(F32)
    out_ref[...] = total.astype(BF16)


def finish_kernel(heads_ref, tokens_ref, out_ref):
    total = tokens_ref[...].astype(F32) + heads_ref[0].astype(F32) + heads_ref[1].astype(F32)
    out_ref[...] = total.astype(BF16)


def call(kernel, shape, *operands):
    out_shape = shape
    if isinstance(shape, tuple):
        out_shape = jax.ShapeDtypeStruct(shape, BF16)
    return pl.pallas_call(
        kernel,
        out_shape=out_shape,
        compiler_params=pltpu.CompilerParams(vmem_limit_bytes=VMEM),
    )(*operands)


def shift(x, axes, count, step):
    return lax.ppermute(x, axes, [(i, (i + step) % count) for i in range(count)])


def by_core(i):
    zf, core = divmod(i, 2)
    return (zf + 1 - 2 * core) % 4 * 2 + core


def together(run, *operands):
    shapes = jax.eval_shape(run, *operands)
    return lax.cond(
        lax.axis_index("za") < 2,
        run,
        lambda *_: jax.tree.map(lambda s: jnp.zeros(s.shape, s.dtype), shapes),
        *operands,
    )


def local(tokens, modulation, w_qkv, w_out, stale, text):
    core = lax.axis_index("core")
    own = stale.reshape(2, BLOCK, 2 * HEAD)
    text = text.reshape(2, -1, 2 * HEAD)
    behind = shift(own, "zf", 4, 1)
    ahead = shift(own, "zf", 4, -1)

    def project(tokens, modulation, w_qkv):
        features = lax.all_to_all(
            jnp.broadcast_to(tokens[None], (PARTS, BLOCK, COLS)), "tensor", 0, 0
        )
        w_qkv = pltpu.with_memory_space_constraint(w_qkv, pltpu.VMEM)
        one_pass = jax.ShapeDtypeStruct((3, BLOCK, HEAD), BF16)
        return call(project_kernel, [one_pass, one_pass], features, modulation, w_qkv)

    own_pass, away = together(project, tokens, modulation, w_qkv)
    away, behind, ahead = lax.optimization_barrier((away, behind, ahead))
    up = jnp.stack([own, behind])
    down = jnp.stack([own, ahead])
    far = lax.ppermute(
        jnp.where(core == 0, behind, ahead), ("zf", "core"), [(i, by_core(i)) for i in range(8)]
    )
    below = shift(up, ("zf", "zb"), 8, 1)
    above = shift(down, ("zf", "zb"), 8, -1)

    def hand_out(own_pass, away):
        heads = lax.all_gather(away, "guidance")
        mine = lax.axis_index("guidance")
        first = jnp.where(mine == 0, own_pass, heads[0])
        second = jnp.where(mine == 0, heads[1], own_pass)
        fresh = jnp.stack([first, second])
        return lax.all_gather(fresh[:, 0], ("za", "core")), fresh

    queries, fresh = together(hand_out, own_pass, away)
    mine = call(
        attend_kernel, (SHARE, REPLY, HEAD), queries, fresh, up, below, above, ahead, far, text
    )
    away = jnp.where(core == 0, mine[1::2], mine[0::2])
    message = call(join_kernel, (2 * CHIPS, LEAF, HEAD), mine, lax.all_gather(away, "core"))
    message = lax.all_to_all(message, ("guidance", "za"), 0, 0)
    parts = call(output_kernel, (PARTS, BLOCK, COLS), message, modulation, w_out)
    parts = lax.all_to_all(parts, "tensor", 0, 0)
    heads = lax.all_gather(call(sum_kernel, (BLOCK, COLS), parts), "guidance")
    return call(finish_kernel, (BLOCK, COLS), heads, tokens)


def solution(mesh):
    fine = jax.sharding.Mesh(
        mesh.devices.reshape(4, 2, 2, 2, 8, 2), ("zf", "zb", "za", "core", "tensor", "guidance")
    )
    patch = ("zf", "zb", "za", "core")
    in_specs = (
        P(patch, "tensor"),
        P(),
        P(None, None, ("tensor", "guidance")),
        P(("tensor", "guidance"), None),
        P(None, "guidance", patch, "tensor"),
        P(None, "guidance", None, "tensor"),
    )
    return jax.shard_map(
        local, mesh=fine, in_specs=in_specs, out_specs=P(patch, "tensor"), check_vma=False
    )
```

time: 172 us -> 102 us (0.59)
  the two profiles are of different devices: /device:TPU:1 before, /device:TPU:64 now
where the time goes in v3:
time: 102 us
  blocking collectives  66.3 us (65%)
  starting transfers between devices  26.9 us (26%)
  Pallas kernels  7.17 us (7%)
  local copies, waits for them, and re-layouts  1.16 us (1%)
    ppermute x4, starting transfers between devices, shift(): lax.ppermute(x, axes, [(i, (i + step) % count) for i in range(count)])  19.6 us
    all_to_all x1, blocking collectives, project(): lax.all_to_all(jnp.broadcast_to(tokens[None], (PARTS, BLOCK, COLS)), 'ten...  17.8 us
    all_to_all x1, blocking collectives, local(): parts = lax.all_to_all(parts, 'tensor', 0, 0)  14.7 us
    all_to_all x1, blocking collectives, local(): message = lax.all_to_all(message, ('guidance', 'za'), 0, 0)  10.8 us
    all_gather x1, blocking collectives, hand_out(): return (lax.all_gather(fresh[:, 0], ('za', 'core')), fresh)  7.41 us
    ppermute x1, starting transfers between devices, local(): lax.ppermute(jnp.where(core == 0, behind, ahead), ('zf', 'core'), [(i, by...  7.28 us
    pallas_call x6, Pallas kernels, call(): pl.pallas_call(kernel, out_shape=out_shape, compiler_params=pltpu.Compile...  7.17 us
    all_gather x1, blocking collectives, hand_out(): heads = lax.all_gather(away, 'guidance')  6.8 us
  transfers between devices with their start and end apart: 5, of which 0 were waited for; matrix products, arithmetic and copies ran while one was open for 1% of the time, Pallas kernels for 2%

profile of v3, /device:TPU:64, one launch (start us, length us, event | category | flops | bytes accessed | tf_op | source)
XLA Modules:
  0.0 101.9 jit_solution(11112941632391923665)
XLA Ops:
  0.0 9.1 %collective-permute-start = (bf16[2,128,256]{2,1,0:T(8,128)(2,1)}, bf16[2,128,256]{2,1,0:T(8,128)(2,1)S(1)}, u32[]{:S(2)}, u32[]{:S(2)}) collective-permute-start(bf16[2,128,256]{2,1,0:T(8,128)(2,1)} %bitcast.18), channel_id=1, source_target_pairs={{0,128},{128,256},{256,384},{384,0},{1,129},{129,257},{257,385},{3... | collective-permute-start | bytes 393224 | tf_op jit(solution)/shard_map/ppermute | solution.py:211
  9.1 3.8 %collective-permute-start.1 = (bf16[2,128,256]{2,1,0:T(8,128)(2,1)}, bf16[2,128,256]{2,1,0:T(8,128)(2,1)S(1)}, u32[]{:S(2)}, u32[]{:S(2)}) collective-permute-start(bf16[2,128,256]{2,1,0:T(8,128)(2,1)} %bitcast.19), channel_id=1, source_target_pairs={{0,384},{128,0},{256,128},{384,256},{1,385},{129,1},{257,129},{385... | collective-permute-start | bytes 393224 | tf_op jit(solution)/shard_map/ppermute | solution.py:211
  12.9 0.0 copy-start.6
  12.9 20.9 %conditional.2 = ((bf16[3,128,128]{2,1,0:T(8,128)(2,1)S(1)}, bf16[3,128,128]{2,1,0:T(8,128)(2,1)S(1)})) conditional(s32[]{:T(128)} %convert_element_type.4, () %tuple.22, (bf16[128,384]{1,0:T(8,128)(2,1)}, f32[3,2,3072]{2,1,0:T(2,128)}, bf16[3,3072,128]{2,1,0:T(8,128)(2,1)}) %tuple.23), branch_computations={%region_0.0_spmd, %region_1.0_spmd} | conditional | bytes 12189760 | solution.py:221
  12.9 0.0 copy-start
  12.9 0.0 copy-start.5
  12.9 1.1 %broadcast_in_dim.0 = bf16[8,128,384]{2,1,0:T(8,128)(2,1)S(1)} broadcast(bf16[128,384]{1,0:T(8,128)(2,1)} %get-tuple-element.15), dimensions={1,2} | broadcast | bytes 884736 | tf_op jit(solution)/shard_map/cond/branch_1_fun/broadcast_in_dim | solution.py:238
  14.0 17.8 %all_to_all.14.x_ref = bf16[8,128,384]{2,1,0:T(8,128)(2,1)S(1)} all-to-all(bf16[8,128,384]{2,1,0:T(8,128)(2,1)S(1)} %broadcast_in_dim.0), channel_id=1, replica_groups=mesh['zf'=4,'zb'=2,'za'=2,'core'=2,'tensor'=8,'guidance'=2] {'tensor'}, dimensions={0} | all-to-all | bytes 1572864 | tf_op jit(solution)/shard_map/cond/branch_1_fun/all_to_all | solution.py:237
  31.8 0.0 copy-done
  31.8 0.0 copy-done.5
  31.8 1.9 %branch_1_fun.1 = (bf16[3,128,128]{2,1,0:T(8,128)(2,1)S(1)}, bf16[3,128,128]{2,1,0:T(8,128)(2,1)S(1)}) custom-call(bf16[8,128,384]{2,1,0:T(8,128)(2,1)S(1)} %all_to_all.14.x_ref, f32[3,2,3072]{2,1,0:T(2,128)S(1)} %copy-done.5, bf16[3,3072,128]{2,1,0:T(8,128)(2,1)S(1)} %copy-done), custom_call_target="tpu_custom_call" | custom-call | tf_op jit(solution)/shard_map/cond/branch_1_fun/pallas_call | solution.py:203
  33.7 0.0 copy-start.2
  33.8 0.0 collective-permute-done
  33.8 0.0 collective-permute-done.1.kv3
  33.8 0.0 copy-done.6
  33.8 4.5 %collective-permute-start.2 = (bf16[2,2,128,256]{3,2,1,0:T(8,128)(2,1)S(1)}, bf16[2,2,128,256]{3,2,1,0:T(8,128)(2,1)S(1)}, u32[]{:S(2)}, u32[]{:S(2)}) collective-permute-start(bf16[2,2,128,256]{3,2,1,0:T(8,128)(2,1)S(1)} %get-tuple-element.39.kv0), channel_id=1, source_target_pairs={{0,64},{64,128},{128,192},{192,256},{256,320},{320,384},{384,448},... | collective-permute-start | bytes 786440 | tf_op jit(solution)/shard_map/ppermute | solution.py:211
  38.4 2.2 %collective-permute-start.3 = (bf16[2,2,128,256]{3,2,1,0:T(8,128)(2,1)S(1)}, bf16[2,2,128,256]{3,2,1,0:T(8,128)(2,1)S(1)}, u32[]{:S(2)}, u32[]{:S(2)}) collective-permute-start(bf16[2,2,128,256]{3,2,1,0:T(8,128)(2,1)S(1)} %get-tuple-element.38), channel_id=1, source_target_pairs={{0,448},{64,0},{128,64},{192,128},{256,192},{320,256},{384,320},{4... | collective-permute-start | bytes 786440 | tf_op jit(solution)/shard_map/ppermute | solution.py:211
  40.6 7.3 %collective-permute-start.4 = (bf16[2,128,256]{2,1,0:T(8,128)(2,1)S(1)}, bf16[2,128,256]{2,1,0:T(8,128)(2,1)S(1)}, u32[]{:S(2)}, u32[]{:S(2)}) collective-permute-start(bf16[2,128,256]{2,1,0:T(8,128)(2,1)S(1)} %broadcast_select_fusion), channel_id=1, source_target_pairs={{0,128},{16,400},{128,256},{144,16},{256,384},{272,144},{384,0},{4... | collective-permute-start | bytes 393224 | tf_op jit(solution)/shard_map/ppermute | solution.py:248
  47.9 14.3 %conditional.3 = (bf16[4,2,128,128]{3,2,1,0:T(8,128)(2,1)S(1)}, bf16[2,3,128,128]{3,2,1,0:T(8,128)(2,1)S(1)}) conditional(s32[]{:T(128)} %convert_element_type.4, () %tuple.21, (bf16[3,128,128]{2,1,0:T(8,128)(2,1)S(1)}, bf16[3,128,128]{2,1,0:T(8,128)(2,1)S(1)}) %tuple.25), branch_computations={%region_2.3_spmd, %region_3.4_spmd} | conditional | flops 229379 | bytes 1769518 | solution.py:221
  47.9 6.8 %all-gather = bf16[6,128,128]{2,1,0:T(8,128)(2,1)S(1)} all-gather(bf16[3,128,128]{2,1,0:T(8,128)(2,1)S(1)} %get-tuple-element.19), channel_id=2, replica_groups=mesh['zf'=4,'zb'=2,'za'=2,'core'=2,'tensor'=8,'guidance'=2] {'guidance'}, dimensions={0}, use_global_device_ids=true | all-gather | bytes 294912 | tf_op jit(solution)/shard_map/cond/branch_1_fun/all_gather | solution.py:255
  54.8 7.4 %all-gather.1 = bf16[8,1,128,128]{3,2,1,0:T(8,128)(2,1)S(1)} all-gather(bf16[2,1,128,128]{3,2,1,0:T(8,128)(2,1)S(1)} %fusion.2), channel_id=3, replica_groups=mesh['zf'=4,'zb'=2,'za'=2,'core'=2,'tensor'=8,'guidance'=2] {'za','core'}, dimensions={0}, use_global_device_ids=true | all-gather | bytes 327680 | tf_op jit(solution)/shard_map/cond/branch_1_fun/all_gather | solution.py:260
  62.2 0.0 copy-start.1
  62.2 0.0 copy-start.4
  62.2 0.0 collective-permute-done.4.kv4
  62.2 0.0 collective-permute-done.2.kv1
  62.2 0.0 collective-permute-done.3.kv2
  62.2 0.0 copy-done.2
  62.3 2.7 %shard_map.65.mine_ref = bf16[4,272,128]{2,1,0:T(8,128)(2,1)S(1)} custom-call(bf16[4,2,128,128]{3,2,1,0:T(8,128)(2,1)S(1)} %get-tuple-element.30.query_ref, bf16[2,3,128,128]{3,2,1,0:T(8,128)(2,1)S(1)} %get-tuple-element.31.fresh_ref, bf16[2,2,128,256]{3,2,1,0:T(8,128)(2,1)S(1)} %get-tuple-element.39.kv0, ...), custom_call_target="tpu_custom_call" | custom-call | tf_op jit(solution)/shard_map/pallas_call | solution.py:203
  64.9 2.0 %all-gather.2 = bf16[4,272,128]{2,1,0:T(8,128)(2,1)S(1)} all-gather(bf16[2,272,128]{2,1,0:T(8,128)(2,1)S(1)} %slice_select_fusion.2), channel_id=4, replica_groups=mesh['zf'=4,'zb'=2,'za'=2,'core'=2,'tensor'=8,'guidance'=2] {'core'}, dimensions={0}, use_global_device_ids=true | all-gather | bytes 417792 | tf_op jit(solution)/shard_map/all_gather | solution.py:267
  66.9 0.8 shard_map.66
  67.7 0.0 copy-start.3
  67.8 10.8 %all_to_all.15.reply_ref = bf16[4,144,128]{2,1,0:T(8,128)(2,1)S(1)} all-to-all(bf16[4,144,128]{2,1,0:T(8,128)(2,1)S(1)} %shard_map.66), channel_id=1, replica_groups=mesh['zf'=4,'zb'=2,'za'=2,'core'=2,'tensor'=8,'guidance'=2] {'guidance',..., dimensions={0} | all-to-all | bytes 294912 | tf_op jit(solution)/shard_map/all_to_all | solution.py:268
  78.6 0.0 copy-done.1
  78.6 0.0 copy-done.4
  78.6 1.0 %shard_map.67 = bf16[8,128,384]{2,1,0:T(8,128)(2,1)S(1)} custom-call(bf16[4,144,128]{2,1,0:T(8,128)(2,1)S(1)} %all_to_all.15.reply_ref, f32[3,2,3072]{2,1,0:T(2,128)S(1)} %copy-done.4, bf16[128,3072]{1,0:T(8,128)(2,1)S(1)} %copy-done.1), custom_call_target="tpu_custom_call" | custom-call | tf_op jit(solution)/shard_map/pallas_call | solution.py:203
  79.6 14.7 %all_to_all.16.parts_ref = bf16[8,128,384]{2,1,0:T(8,128)(2,1)S(1)} all-to-all(bf16[8,128,384]{2,1,0:T(8,128)(2,1)S(1)} %shard_map.67), channel_id=1, replica_groups=mesh['zf'=4,'zb'=2,'za'=2,'core'=2,'tensor'=8,'guidance'=2] {'tensor'}, dimensions={0} | all-to-all | bytes 1572864 | tf_op jit(solution)/shard_map/all_to_all | solution.py:270
  94.3 0.1 shard_map.68
  94.4 6.8 %all-gather.3 = bf16[256,384]{1,0:T(8,128)(2,1)S(1)} all-gather(bf16[128,384]{1,0:T(8,128)(2,1)S(1)} %shard_map.68), channel_id=5, replica_groups=mesh['zf'=4,'zb'=2,'za'=2,'core'=2,'tensor'=8,'guidance'=2] {'guidance'}, dimensions={0}, use_global_device_ids=true | all-gather | bytes 294912 | tf_op jit(solution)/shard_map/all_gather | solution.py:271
  101.2 0.0 copy-done.3
  101.2 0.7 shard_map.69
  (6 shorter events, 0.1 us)
Async XLA Ops:
  0.0 33.8 %collective-permute-start = (bf16[2,128,256]{2,1,0:T(8,128)(2,1)}, bf16[2,128,256]{2,1,0:T(8,128)(2,1)S(1)}, u32[]{:S(2)}, u32[]{:S(2)}) collective-permute-start(bf16[2,128,256]{2,1,0:T(8,128)(2,1)} %bitcast.18), channel_id=1, source_target_pairs={{0,128},{128,256},{256,384},{384,0},{1,129},{129,257},{257,385},{3... | collective-permute-start | bytes 393224 | tf_op jit(solution)/shard_map/ppermute | solution.py:211
  9.1 24.7 %collective-permute-start.1 = (bf16[2,128,256]{2,1,0:T(8,128)(2,1)}, bf16[2,128,256]{2,1,0:T(8,128)(2,1)S(1)}, u32[]{:S(2)}, u32[]{:S(2)}) collective-permute-start(bf16[2,128,256]{2,1,0:T(8,128)(2,1)} %bitcast.19), channel_id=1, source_target_pairs={{0,384},{128,0},{256,128},{384,256},{1,385},{129,1},{257,129},{385... | collective-permute-start | bytes 393224 | tf_op jit(solution)/shard_map/ppermute | solution.py:211
  12.9 20.9 %copy-start.6 = (bf16[2,1,128,256]{3,2,1,0:T(8,128)(2,1)S(1)}, bf16[2,1,128,256]{3,2,1,0:T(8,128)(2,1)}, u32[]{:S(2)}) copy-start(bf16[2,1,128,256]{3,2,1,0:T(8,128)(2,1)} %param.14) | copy-start | bytes 393220
  12.9 18.9 %copy-start = (bf16[3,3072,128]{2,1,0:T(8,128)(2,1)S(1)}, bf16[3,3072,128]{2,1,0:T(8,128)(2,1)}, u32[]{:S(2)}) copy-start(bf16[3,3072,128]{2,1,0:T(8,128)(2,1)} %get-tuple-element.35.w_ref) | copy-start | bytes 7077892 | tf_op jit(solution)/shard_map/cond
  12.9 18.9 %copy-start.5 = (f32[3,2,3072]{2,1,0:T(2,128)S(1)}, f32[3,2,3072]{2,1,0:T(2,128)}, u32[]{:S(2)}) copy-start(f32[3,2,3072]{2,1,0:T(2,128)} %get-tuple-element.16.mod_ref) | copy-start | bytes 221188 | tf_op jit(solution)/shard_map/cond
  33.7 28.5 %copy-start.2 = (bf16[2,1,256,256]{3,2,1,0:T(8,128)(2,1)S(1)}, bf16[2,1,256,256]{3,2,1,0:T(8,128)(2,1)}, u32[]{:S(2)}) copy-start(bf16[2,1,256,256]{3,2,1,0:T(8,128)(2,1)} %param.15) | copy-start | bytes 786436
  33.8 28.4 %collective-permute-start.2 = (bf16[2,2,128,256]{3,2,1,0:T(8,128)(2,1)S(1)}, bf16[2,2,128,256]{3,2,1,0:T(8,128)(2,1)S(1)}, u32[]{:S(2)}, u32[]{:S(2)}) collective-permute-start(bf16[2,2,128,256]{3,2,1,0:T(8,128)(2,1)S(1)} %get-tuple-element.39.kv0), channel_id=1, source_target_pairs={{0,64},{64,128},{128,192},{192,256},{256,320},{320,384},{384,448},... | collective-permute-start | bytes 786440 | tf_op jit(solution)/shard_map/ppermute | solution.py:211
  38.4 23.8 %collective-permute-start.3 = (bf16[2,2,128,256]{3,2,1,0:T(8,128)(2,1)S(1)}, bf16[2,2,128,256]{3,2,1,0:T(8,128)(2,1)S(1)}, u32[]{:S(2)}, u32[]{:S(2)}) collective-permute-start(bf16[2,2,128,256]{3,2,1,0:T(8,128)(2,1)S(1)} %get-tuple-element.38), channel_id=1, source_target_pairs={{0,448},{64,0},{128,64},{192,128},{256,192},{320,256},{384,320},{4... | collective-permute-start | bytes 786440 | tf_op jit(solution)/shard_map/ppermute | solution.py:211
  40.6 21.6 %collective-permute-start.4 = (bf16[2,128,256]{2,1,0:T(8,128)(2,1)S(1)}, bf16[2,128,256]{2,1,0:T(8,128)(2,1)S(1)}, u32[]{:S(2)}, u32[]{:S(2)}) collective-permute-start(bf16[2,128,256]{2,1,0:T(8,128)(2,1)S(1)} %broadcast_select_fusion), channel_id=1, source_target_pairs={{0,128},{16,400},{128,256},{144,16},{256,384},{272,144},{384,0},{4... | collective-permute-start | bytes 393224 | tf_op jit(solution)/shard_map/ppermute | solution.py:248
  62.2 16.4 %copy-start.1 = (bf16[128,3072]{1,0:T(8,128)(2,1)S(1)}, bf16[128,3072]{1,0:T(8,128)(2,1)}, u32[]{:S(2)}) copy-start(bf16[128,3072]{1,0:T(8,128)(2,1)} %w_ref.1) | copy-start | bytes 2359300
  62.2 16.4 %copy-start.4 = (f32[3,2,3072]{2,1,0:T(2,128)S(1)}, f32[3,2,3072]{2,1,0:T(2,128)}, u32[]{:S(2)}) copy-start(f32[3,2,3072]{2,1,0:T(2,128)} %mod_ref.1) | copy-start | bytes 221188
  67.7 33.5 %copy-start.3 = (bf16[128,384]{1,0:T(8,128)(2,1)S(1)}, bf16[128,384]{1,0:T(8,128)(2,1)}, u32[]{:S(2)}) copy-start(bf16[128,384]{1,0:T(8,128)(2,1)} %tokens_ref.1) | copy-start | bytes 294916

commit v4 on v3

--- a/solution.py
+++ b/solution.py
@@ -16,10 +16,8 @@
 PARTS = 8
 COLS = 384
 SHARE = 4
-CHIPS = 2
 QUERIES = SHARE * BLOCK
 LEAF = BLOCK + 16
-REPLY = 2 * BLOCK + 16
 BF16 = jnp.bfloat16
 F32 = jnp.float32
 VMEM = 24 * 1024 * 1024
@@ -81,31 +79,20 @@
     return high, middle, level - high - middle
 
 
-def read_levels(stats):
-    count = sum(s.shape[0] for s in stats) // 16
-    stats = [s.astype(F32) for s in stats] + [jnp.zeros((HEAD - 16 * count, HEAD), F32)]
-    stats = jnp.transpose(jnp.concatenate(stats, axis=0))
-    return [
-        [sum(stats[:, 16 * j + 3 * h + i : 16 * j + 3 * h + i + 1] for i in range(3)) for h in range(2)]
-        for j in range(count)
-    ]
-
-
 def join(levels, parts):
-    top = jnp.maximum(levels[0], levels[1])
+    top = levels[0]
+    for level in levels[1:]:
+        top = jnp.maximum(top, level)
     shares = [jnp.exp2(level - top) for level in levels]
-    total = shares[0] + shares[1]
-    joined = shares[0] * parts[0].astype(F32) + shares[1] * parts[1].astype(F32)
-    return joined / total, top + jnp.log2(total)
-
-
-def attend_kernel(query_ref, fresh_ref, kv0, kv1, kv2, kv3, kv4, text_ref, out_ref):
+    joined = sum(share * part.astype(F32) for share, part in zip(shares, parts))
+    return joined / sum(shares)
+
+
+def attend_kernel(query_ref, fresh_ref, own_ref, far_ref, near_ref, next_ref, mid_ref, text_ref, out_ref):
     own = lax.axis_index("za") * 2 + lax.axis_index("core")
     text_rows = text_ref.shape[1] // SHARE
     first = pl.multiple_of(own * text_rows, text_rows)
     row_block = lax.broadcasted_iota(jnp.int32, (QUERIES, 1), 0) // BLOCK
-    col = lax.broadcasted_iota(jnp.int32, (1, 2 * BLOCK), 1)
-    own_stale = (row_block == own) & (col < BLOCK)
     other_rows = row_block != own
     lane = lax.broadcasted_iota(jnp.int32, (1, HEAD), 1)
     stats = jnp.zeros((BLOCK, HEAD), F32)
@@ -113,15 +100,13 @@
         cols = slice(h * HEAD, (h + 1) * HEAD)
         query = query_ref[:, h].reshape(QUERIES, HEAD)
         scores, values = [], []
-        for n, kv in enumerate((kv0, kv1, kv2)):
-            s = nt(query, kv[:, 0, :, cols].reshape(2 * BLOCK, HEAD))
-            if n == 0:
-                s = jnp.where(own_stale, NEGATIVE, s)
-            scores.append(s)
-            values.append(kv[:, 1, :, cols].reshape(2 * BLOCK, HEAD))
-        for kv in (kv3, kv4):
+        for kv in (own_ref, far_ref):
             scores.append(nt(query, kv[0, :, cols]))
             values.append(kv[1, :, cols])
+        scores[0] = jnp.where(other_rows, scores[0], NEGATIVE)
+        for kv in (near_ref, next_ref, mid_ref):
+            scores.append(nt(query, kv[:, 0, :, cols].reshape(2 * BLOCK, HEAD)))
+            values.append(kv[:, 1, :, cols].reshape(2 * BLOCK, HEAD))
         scores.append(jnp.where(other_rows, NEGATIVE, nt(query, fresh_ref[h, 1])))
         values.append(fresh_ref[h, 2])
         scores.append(nt(query, text_ref[0, pl.ds(first, text_rows), cols]))
@@ -139,42 +124,22 @@
         pieces = split_level(top + jnp.log2(total))
         for b in range(SHARE):
             rows = slice(b * BLOCK, (b + 1) * BLOCK)
-            out_ref[b, h * BLOCK : (h + 1) * BLOCK, :] = summed[rows]
+            out_ref[h * SHARE + b, 0:BLOCK, :] = summed[rows]
             for i, piece in enumerate(pieces):
-                stats = jnp.where(lane == 16 * b + 3 * h + i, piece[rows], stats)
+                stats = jnp.where(lane == 16 * (h * SHARE + b) + i, piece[rows], stats)
     stats = jnp.transpose(stats).astype(BF16)
-    for b in range(SHARE):
-        out_ref[b, 2 * BLOCK : REPLY, :] = stats[16 * b : 16 * b + 16]
-
-
-def join_kernel(mine_ref, cores_ref, out_ref):
-    core = lax.axis_index("core")
-    lane = lax.broadcasted_iota(jnp.int32, (1, HEAD), 1)
-    stats = jnp.zeros((BLOCK, HEAD), F32)
-    mine = [mine_ref[pl.ds(2 * b + core, 1)][0] for b in range(CHIPS)]
-    other = [cores_ref[pl.ds(1 - core, 1), b][0] for b in range(CHIPS)]
-    levels = read_levels([m[2 * BLOCK : REPLY] for m in mine + other])
-    for b in range(CHIPS):
-        for h in range(2):
-            rows = slice(h * BLOCK, (h + 1) * BLOCK)
-            joined, level = join(
-                [levels[b][h], levels[CHIPS + b][h]], [mine[b][rows], other[b][rows]]
-            )
-            out_ref[h * CHIPS + b, 0:BLOCK, :] = joined.astype(BF16)
-            for i, piece in enumerate(split_level(level)):
-                stats = jnp.where(lane == 16 * (h * CHIPS + b) + i, piece, stats)
-    stats = jnp.transpose(stats).astype(BF16)
-    for d in range(2 * CHIPS):
+    for d in range(2 * SHARE):
         out_ref[d, BLOCK:LEAF, :] = stats[16 * d : 16 * d + 16]
 
 
 def output_kernel(reply_ref, mod_ref, w_ref, out_ref):
-    levels = read_levels([reply_ref[s, BLOCK:LEAF, :] for s in range(2 * CHIPS)])
+    stats = [reply_ref[s, BLOCK:LEAF, :].astype(F32) for s in range(2 * SHARE)]
+    stats = jnp.transpose(jnp.concatenate(stats, axis=0))
     attended = []
     for p in range(2):
-        pair = (p * CHIPS, p * CHIPS + 1)
-        joined, _ = join([levels[s][0] for s in pair], [reply_ref[s, 0:BLOCK, :] for s in pair])
-        attended.append(joined.astype(BF16))
+        four = range(p * SHARE, (p + 1) * SHARE)
+        levels = [sum(stats[:, 16 * s + i : 16 * s + i + 1] for i in range(3)) for s in four]
+        attended.append(join(levels, [reply_ref[s, 0:BLOCK, :] for s in four]).astype(BF16))
     attended = jnp.concatenate(attended, axis=0)
     for b in range(PARTS):
         cols = slice(b * COLS, (b + 1) * COLS)
@@ -207,13 +172,12 @@
     )(*operands)
 
 
-def shift(x, axes, count, step):
-    return lax.ppermute(x, axes, [(i, (i + step) % count) for i in range(count)])
-
-
-def by_core(i):
-    zf, core = divmod(i, 2)
-    return (zf + 1 - 2 * core) % 4 * 2 + core
+def by_core(count):
+    return [
+        (2 * i + core, 2 * ((i + 1 - 2 * core) % count) + core)
+        for i in range(count)
+        for core in range(2)
+    ]
 
 
 def together(run, *operands):
@@ -230,8 +194,9 @@
     core = lax.axis_index("core")
     own = stale.reshape(2, BLOCK, 2 * HEAD)
     text = text.reshape(2, -1, 2 * HEAD)
-    behind = shift(own, "zf", 4, 1)
-    ahead = shift(own, "zf", 4, -1)
+    chip = lax.all_gather(own, "core")
+    near = lax.ppermute(chip, ("zf", "core"), by_core(4))
+    beside = lax.ppermute(chip, ("zf", "zb", "core"), by_core(8))
 
     def project(tokens, modulation, w_qkv):
         features = lax.all_to_all(
@@ -242,14 +207,9 @@
         return call(project_kernel, [one_pass, one_pass], features, modulation, w_qkv)
 
     own_pass, away = together(project, tokens, modulation, w_qkv)
-    away, behind, ahead = lax.optimization_barrier((away, behind, ahead))
-    up = jnp.stack([own, behind])
-    down = jnp.stack([own, ahead])
-    far = lax.ppermute(
-        jnp.where(core == 0, behind, ahead), ("zf", "core"), [(i, by_core(i)) for i in range(8)]
-    )
-    below = shift(up, ("zf", "zb"), 8, 1)
-    above = shift(down, ("zf", "zb"), 8, -1)
+    away, near, beside = lax.optimization_barrier((away, near, beside))
+    mid = lax.ppermute(near, ("zf", "zb", "core"), by_core(8))
+    far = lax.ppermute(jnp.where(core == 0, near[0], near[1]), ("zf", "core"), by_core(4))
 
     def hand_out(own_pass, away):
         heads = lax.all_gather(away, "guidance")
@@ -260,12 +220,10 @@
         return lax.all_gather(fresh[:, 0], ("za", "core")), fresh
 
     queries, fresh = together(hand_out, own_pass, away)
-    mine = call(
-        attend_kernel, (SHARE, REPLY, HEAD), queries, fresh, up, below, above, ahead, far, text
-    )
-    away = jnp.where(core == 0, mine[1::2], mine[0::2])
-    message = call(join_kernel, (2 * CHIPS, LEAF, HEAD), mine, lax.all_gather(away, "core"))
-    message = lax.all_to_all(message, ("guidance", "za"), 0, 0)
+    message = call(
+        attend_kernel, (2 * SHARE, LEAF, HEAD), queries, fresh, own, far, near, beside, mid, text
+    )
+    message = lax.all_to_all(message, ("guidance", "za", "core"), 0, 0)
     parts = call(output_kernel, (PARTS, BLOCK, COLS), message, modulation, w_out)
     parts = lax.all_to_all(parts, "tensor", 0, 0)
     heads = lax.all_gather(call(sum_kernel, (BLOCK, COLS), parts), "guidance")

time: 102 us -> 99.8 us (0.978)
  the two profiles are of different devices: /device:TPU:64 before, /device:TPU:1 now
where the time goes in v4:
time: 99.8 us; the launch traced here: 98.7 us
  blocking collectives  74 us (74%)
  starting transfers between devices  16.8 us (17%)
  Pallas kernels  6.45 us (6%)
  local copies, waits for them, and re-layouts  1.15 us (1%)
    all_to_all x1, blocking collectives, project(): lax.all_to_all(jnp.broadcast_to(tokens[None], (PARTS, BLOCK, COLS)), 'ten...  16.8 us
    all_to_all x1, blocking collectives, local(): parts = lax.all_to_all(parts, 'tensor', 0, 0)  14.5 us
    all_to_all x1, blocking collectives, local(): message = lax.all_to_all(message, ('guidance', 'za', 'core'), 0, 0)  12.9 us
    all_gather x1, blocking collectives, hand_out(): return (lax.all_gather(fresh[:, 0], ('za', 'core')), fresh)  9.34 us
    all_gather x1, blocking collectives, local(): chip = lax.all_gather(own, 'core')  8.71 us
    ppermute x1, starting transfers between devices, local(): near = lax.ppermute(chip, ('zf', 'core'), by_core(4))  7.07 us
    pallas_call x5, Pallas kernels, call(): pl.pallas_call(kernel, out_shape=out_shape, compiler_params=pltpu.Compile...  6.45 us
    all_gather x1, blocking collectives, hand_out(): heads = lax.all_gather(away, 'guidance')  6.07 us
  transfers between devices with their start and end apart: 4, of which 0 were waited for; matrix products, arithmetic and copies ran while one was open for 1% of the time, Pallas kernels for 2%

profile of v4, /device:TPU:1, one launch (start us, length us, event | category | flops | bytes accessed | tf_op | source)
XLA Modules:
  0.0 98.7 jit_solution(13601228244020490694)
XLA Ops:
  0.0 8.7 %all-gather.2 = bf16[4,1,128,256]{3,2,1,0:T(8,128)(2,1)S(1)} all-gather(bf16[2,1,128,256]{3,2,1,0:T(8,128)(2,1)} %param.14), channel_id=4, replica_groups=mesh['zf'=4,'zb'=2,'za'=2,'core'=2,'tensor'=8,'guidance'=2] {'core'}, dimensions={0}, use_global_device_ids=true | all-gather | bytes 393216 | tf_op jit(solution)/shard_map/all_gather | solution.py:197
  8.7 7.1 %collective-permute-start = (bf16[2,2,128,256]{3,2,1,0:T(8,128)(2,1)S(1)}, bf16[2,2,128,256]{3,2,1,0:T(8,128)(2,1)S(1)}, u32[]{:S(2)}, u32[]{:S(2)}) collective-permute-start(bf16[2,2,128,256]{3,2,1,0:T(8,128)(2,1)S(1)} %bitcast.15), channel_id=1, source_target_pairs={{0,128},{16,400},{128,256},{144,16},{256,384},{272,144},{384,0},{4... | collective-permute-start | bytes 786440 | tf_op jit(solution)/shard_map/ppermute | solution.py:198
  15.8 4.3 %collective-permute-start.1 = (bf16[2,2,128,256]{3,2,1,0:T(8,128)(2,1)S(1)}, bf16[2,2,128,256]{3,2,1,0:T(8,128)(2,1)S(1)}, u32[]{:S(2)}, u32[]{:S(2)}) collective-permute-start(bf16[2,2,128,256]{3,2,1,0:T(8,128)(2,1)S(1)} %bitcast.16), channel_id=1, source_target_pairs={{0,64},{16,464},{64,128},{80,16},{128,192},{144,80},{192,256},{208... | collective-permute-start | bytes 786440 | tf_op jit(solution)/shard_map/ppermute | solution.py:199
  20.1 19.9 %conditional.2 = ((bf16[3,128,128]{2,1,0:T(8,128)(2,1)S(1)}, bf16[3,128,128]{2,1,0:T(8,128)(2,1)S(1)})) conditional(s32[]{:T(128)} %convert_element_type.4, () %tuple.22, (bf16[128,384]{1,0:T(8,128)(2,1)}, f32[3,2,3072]{2,1,0:T(2,128)}, bf16[3,3072,128]{2,1,0:T(8,128)(2,1)}) %tuple.23), branch_computations={%region_0.0_spmd, %region_1.0_spmd} | conditional | bytes 12189760 | solution.py:185
  20.1 0.0 copy-start
  20.1 0.0 copy-start.6
  20.1 1.1 %broadcast_in_dim.0 = bf16[8,128,384]{2,1,0:T(8,128)(2,1)S(1)} broadcast(bf16[128,384]{1,0:T(8,128)(2,1)} %get-tuple-element.15), dimensions={1,2} | broadcast | bytes 884736 | tf_op jit(solution)/shard_map/cond/branch_1_fun/broadcast_in_dim | solution.py:203
  21.2 16.8 %all_to_all.14.x_ref = bf16[8,128,384]{2,1,0:T(8,128)(2,1)S(1)} all-to-all(bf16[8,128,384]{2,1,0:T(8,128)(2,1)S(1)} %broadcast_in_dim.0), channel_id=1, replica_groups=mesh['zf'=4,'zb'=2,'za'=2,'core'=2,'tensor'=8,'guidance'=2] {'tensor'}, dimensions={0} | all-to-all | bytes 1572864 | tf_op jit(solution)/shard_map/cond/branch_1_fun/all_to_all | solution.py:202
  38.0 0.0 copy-done
  38.0 0.0 copy-done.6
  38.0 1.9 %branch_1_fun.1 = (bf16[3,128,128]{2,1,0:T(8,128)(2,1)S(1)}, bf16[3,128,128]{2,1,0:T(8,128)(2,1)S(1)}) custom-call(bf16[8,128,384]{2,1,0:T(8,128)(2,1)S(1)} %all_to_all.14.x_ref, f32[3,2,3072]{2,1,0:T(2,128)S(1)} %copy-done.6, bf16[3,3072,128]{2,1,0:T(8,128)(2,1)S(1)} %copy-done), custom_call_target="tpu_custom_call" | custom-call | tf_op jit(solution)/shard_map/cond/branch_1_fun/pallas_call | solution.py:168
  40.0 0.0 copy-start.2
  40.0 0.0 copy-start.3
  40.0 0.0 collective-permute-done.near_ref
  40.0 0.0 collective-permute-done.1.next_ref
  40.0 2.5 %collective-permute-start.3 = (bf16[2,2,128,256]{3,2,1,0:T(8,128)(2,1)S(1)}, bf16[2,2,128,256]{3,2,1,0:T(8,128)(2,1)S(1)}, u32[]{:S(2)}, u32[]{:S(2)}) collective-permute-start(bf16[2,2,128,256]{3,2,1,0:T(8,128)(2,1)S(1)} %collective-permute-done.near_ref), channel_id=1, source_target_pairs={{0,64},{16,464},{64,128},{80,16},{128,192},{144,80},{192,256},{208... | collective-permute-start | bytes 786440 | tf_op jit(solution)/shard_map/ppermute | solution.py:211
  42.6 2.9 %collective-permute-start.2 = (bf16[2,128,256]{2,1,0:T(8,128)(2,1)S(1)}, bf16[2,128,256]{2,1,0:T(8,128)(2,1)S(1)}, u32[]{:S(2)}, u32[]{:S(2)}) collective-permute-start(bf16[2,128,256]{2,1,0:T(8,128)(2,1)S(1)} %select_bitcast_fusion), channel_id=1, source_target_pairs={{0,128},{16,400},{128,256},{144,16},{256,384},{272,144},{384,0},{4... | collective-permute-start | bytes 393224 | tf_op jit(solution)/shard_map/ppermute | solution.py:212
  45.5 0.0 copy-start.1
  45.5 0.0 copy-start.5
  45.5 15.5 %conditional.3 = (bf16[4,2,128,128]{3,2,1,0:T(8,128)(2,1)S(1)}, bf16[2,3,128,128]{3,2,1,0:T(8,128)(2,1)S(1)}) conditional(s32[]{:T(128)} %convert_element_type.4, () %tuple.21, (bf16[3,128,128]{2,1,0:T(8,128)(2,1)S(1)}, bf16[3,128,128]{2,1,0:T(8,128)(2,1)S(1)}) %tuple.25), branch_computations={%region_2.3_spmd, %region_3.4_spmd} | conditional | flops 229379 | bytes 1769518 | solution.py:185
  45.5 6.1 %all-gather = bf16[6,128,128]{2,1,0:T(8,128)(2,1)S(1)} all-gather(bf16[3,128,128]{2,1,0:T(8,128)(2,1)S(1)} %get-tuple-element.19), channel_id=2, replica_groups=mesh['zf'=4,'zb'=2,'za'=2,'core'=2,'tensor'=8,'guidance'=2] {'guidance'}, dimensions={0}, use_global_device_ids=true | all-gather | bytes 294912 | tf_op jit(solution)/shard_map/cond/branch_1_fun/all_gather | solution.py:215
  51.7 9.3 %all-gather.1 = bf16[8,1,128,128]{3,2,1,0:T(8,128)(2,1)S(1)} all-gather(bf16[2,1,128,128]{3,2,1,0:T(8,128)(2,1)S(1)} %fusion.2), channel_id=3, replica_groups=mesh['zf'=4,'zb'=2,'za'=2,'core'=2,'tensor'=8,'guidance'=2] {'za','core'}, dimensions={0}, use_global_device_ids=true | all-gather | bytes 327680 | tf_op jit(solution)/shard_map/cond/branch_1_fun/all_gather | solution.py:220
  61.0 0.0 collective-permute-done.2.far_ref
  61.0 0.0 collective-permute-done.3.mid_ref
  61.0 0.0 copy-done.2
  61.0 0.0 copy-done.3
  61.0 2.6 %shard_map.65 = bf16[8,144,128]{2,1,0:T(8,128)(2,1)S(1)} custom-call(bf16[4,2,128,128]{3,2,1,0:T(8,128)(2,1)S(1)} %get-tuple-element.30.query_ref, bf16[2,3,128,128]{3,2,1,0:T(8,128)(2,1)S(1)} %get-tuple-element.31.fresh_ref, bf16[2,128,256]{2,1,0:T(8,128)(2,1)S(1)} %bitcast.12, bf16[2,128,256]{2,1,0:T(8,128)(2,1)S(1)} %collective-permute-done.2.far_ref, ...), custom_call_target="tpu_custom_call" | custom-call | tf_op jit(solution)/shard_map/pallas_call | solution.py:168
  63.6 12.9 %all_to_all.15.reply_ref = bf16[8,144,128]{2,1,0:T(8,128)(2,1)S(1)} all-to-all(bf16[8,144,128]{2,1,0:T(8,128)(2,1)S(1)} %shard_map.65), channel_id=1, replica_groups=mesh['zf'=4,'zb'=2,'za'=2,'core'=2,'tensor'=8,'guidance'=2] {'guidance',..., dimensions={0} | all-to-all | bytes 589824 | tf_op jit(solution)/shard_map/all_to_all | solution.py:226
  76.5 0.0 copy-done.1
  76.5 0.0 copy-done.5
  76.5 0.0 copy-start.4
  76.5 1.2 %shard_map.66 = bf16[8,128,384]{2,1,0:T(8,128)(2,1)S(1)} custom-call(bf16[8,144,128]{2,1,0:T(8,128)(2,1)S(1)} %all_to_all.15.reply_ref, f32[3,2,3072]{2,1,0:T(2,128)S(1)} %copy-done.5, bf16[128,3072]{1,0:T(8,128)(2,1)S(1)} %copy-done.1), custom_call_target="tpu_custom_call" | custom-call | tf_op jit(solution)/shard_map/pallas_call | solution.py:168
  77.7 14.5 %all_to_all.16.parts_ref = bf16[8,128,384]{2,1,0:T(8,128)(2,1)S(1)} all-to-all(bf16[8,128,384]{2,1,0:T(8,128)(2,1)S(1)} %shard_map.66), channel_id=1, replica_groups=mesh['zf'=4,'zb'=2,'za'=2,'core'=2,'tensor'=8,'guidance'=2] {'tensor'}, dimensions={0} | all-to-all | bytes 1572864 | tf_op jit(solution)/shard_map/all_to_all | solution.py:228
  92.2 0.1 shard_map.67
  92.3 5.6 %all-gather.3 = bf16[256,384]{1,0:T(8,128)(2,1)S(1)} all-gather(bf16[128,384]{1,0:T(8,128)(2,1)S(1)} %shard_map.67), channel_id=5, replica_groups=mesh['zf'=4,'zb'=2,'za'=2,'core'=2,'tensor'=8,'guidance'=2] {'guidance'}, dimensions={0}, use_global_device_ids=true | all-gather | bytes 294912 | tf_op jit(solution)/shard_map/all_gather | solution.py:229
  98.0 0.0 copy-done.4
  98.0 0.7 shard_map.68
  (4 shorter events, 0.1 us)
Async XLA Ops:
  8.7 31.3 %collective-permute-start = (bf16[2,2,128,256]{3,2,1,0:T(8,128)(2,1)S(1)}, bf16[2,2,128,256]{3,2,1,0:T(8,128)(2,1)S(1)}, u32[]{:S(2)}, u32[]{:S(2)}) collective-permute-start(bf16[2,2,128,256]{3,2,1,0:T(8,128)(2,1)S(1)} %bitcast.15), channel_id=1, source_target_pairs={{0,128},{16,400},{128,256},{144,16},{256,384},{272,144},{384,0},{4... | collective-permute-start | bytes 786440 | tf_op jit(solution)/shard_map/ppermute | solution.py:198
  15.8 24.2 %collective-permute-start.1 = (bf16[2,2,128,256]{3,2,1,0:T(8,128)(2,1)S(1)}, bf16[2,2,128,256]{3,2,1,0:T(8,128)(2,1)S(1)}, u32[]{:S(2)}, u32[]{:S(2)}) collective-permute-start(bf16[2,2,128,256]{3,2,1,0:T(8,128)(2,1)S(1)} %bitcast.16), channel_id=1, source_target_pairs={{0,64},{16,464},{64,128},{80,16},{128,192},{144,80},{192,256},{208... | collective-permute-start | bytes 786440 | tf_op jit(solution)/shard_map/ppermute | solution.py:199
  20.1 17.9 %copy-start = (bf16[3,3072,128]{2,1,0:T(8,128)(2,1)S(1)}, bf16[3,3072,128]{2,1,0:T(8,128)(2,1)}, u32[]{:S(2)}) copy-start(bf16[3,3072,128]{2,1,0:T(8,128)(2,1)} %get-tuple-element.35.w_ref) | copy-start | bytes 7077892 | tf_op jit(solution)/shard_map/cond
  20.1 17.9 %copy-start.6 = (f32[3,2,3072]{2,1,0:T(2,128)S(1)}, f32[3,2,3072]{2,1,0:T(2,128)}, u32[]{:S(2)}) copy-start(f32[3,2,3072]{2,1,0:T(2,128)} %get-tuple-element.16.mod_ref) | copy-start | bytes 221188 | tf_op jit(solution)/shard_map/cond
  40.0 21.1 %copy-start.2 = (bf16[2,1,128,256]{3,2,1,0:T(8,128)(2,1)S(1)}, bf16[2,1,128,256]{3,2,1,0:T(8,128)(2,1)}, u32[]{:S(2)}) copy-start(bf16[2,1,128,256]{3,2,1,0:T(8,128)(2,1)} %param.14) | copy-start | bytes 393220
  40.0 21.1 %copy-start.3 = (bf16[2,1,256,256]{3,2,1,0:T(8,128)(2,1)S(1)}, bf16[2,1,256,256]{3,2,1,0:T(8,128)(2,1)}, u32[]{:S(2)}) copy-start(bf16[2,1,256,256]{3,2,1,0:T(8,128)(2,1)} %param.15) | copy-start | bytes 786436
  40.0 21.0 %collective-permute-start.3 = (bf16[2,2,128,256]{3,2,1,0:T(8,128)(2,1)S(1)}, bf16[2,2,128,256]{3,2,1,0:T(8,128)(2,1)S(1)}, u32[]{:S(2)}, u32[]{:S(2)}) collective-permute-start(bf16[2,2,128,256]{3,2,1,0:T(8,128)(2,1)S(1)} %collective-permute-done.near_ref), channel_id=1, source_target_pairs={{0,64},{16,464},{64,128},{80,16},{128,192},{144,80},{192,256},{208... | collective-permute-start | bytes 786440 | tf_op jit(solution)/shard_map/ppermute | solution.py:211
  42.6 18.4 %collective-permute-start.2 = (bf16[2,128,256]{2,1,0:T(8,128)(2,1)S(1)}, bf16[2,128,256]{2,1,0:T(8,128)(2,1)S(1)}, u32[]{:S(2)}, u32[]{:S(2)}) collective-permute-start(bf16[2,128,256]{2,1,0:T(8,128)(2,1)S(1)} %select_bitcast_fusion), channel_id=1, source_target_pairs={{0,128},{16,400},{128,256},{144,16},{256,384},{272,144},{384,0},{4... | collective-permute-start | bytes 393224 | tf_op jit(solution)/shard_map/ppermute | solution.py:212
  45.5 31.0 %copy-start.1 = (bf16[128,3072]{1,0:T(8,128)(2,1)S(1)}, bf16[128,3072]{1,0:T(8,128)(2,1)}, u32[]{:S(2)}) copy-start(bf16[128,3072]{1,0:T(8,128)(2,1)} %w_ref.1) | copy-start | bytes 2359300
  45.5 31.0 %copy-start.5 = (f32[3,2,3072]{2,1,0:T(2,128)S(1)}, f32[3,2,3072]{2,1,0:T(2,128)}, u32[]{:S(2)}) copy-start(f32[3,2,3072]{2,1,0:T(2,128)} %mod_ref.1) | copy-start | bytes 221188
  76.5 21.5 %copy-start.4 = (bf16[128,384]{1,0:T(8,128)(2,1)S(1)}, bf16[128,384]{1,0:T(8,128)(2,1)}, u32[]{:S(2)}) copy-start(bf16[128,384]{1,0:T(8,128)(2,1)} %tokens_ref.1) | copy-start | bytes 294916

commit v5 on v4

--- a/solution.py
+++ b/solution.py
@@ -10,7 +10,6 @@
 HEAD = 128
 GUIDE = 3.0
 EPSILON = 1e-06
-NEGATIVE = -1e30
 BASE = math.log2(math.e) / math.sqrt(HEAD)
 BLOCK = 128
 PARTS = 8
@@ -41,7 +40,7 @@
         centered = x_ref[b].astype(F32) - average
         total += jnp.sum(centered * centered, axis=-1, keepdims=True)
     inverse = lax.rsqrt(total * (1.0 / (PARTS * COLS)) + EPSILON)
-    sums = [jnp.zeros((2 * BLOCK, HEAD), F32) for _ in range(3)]
+    sums = jnp.zeros((2 * BLOCK, 3 * HEAD), F32)
     for b in range(PARTS):
         cols = slice(b * COLS, (b + 1) * COLS)
         normed = (x_ref[b].astype(F32) - average) * inverse
@@ -50,8 +49,8 @@
             for p in range(2)
         ]
         both = jnp.concatenate(both, axis=0)
-        for i in range(3):
-            sums[i] += nn(both, w_ref[i, cols, :])
+        sums += nn(both, jnp.concatenate([w_ref[i, cols, :] for i in range(3)], axis=1))
+    sums = [sums[:, i * HEAD : (i + 1) * HEAD] for i in range(3)]
 
     def head_norm(v, scale):
         inverse = lax.rsqrt(jnp.mean(v * v, axis=-1, keepdims=True) + EPSILON) * scale
@@ -99,16 +98,12 @@
     for h in range(2):
         cols = slice(h * HEAD, (h + 1) * HEAD)
         query = query_ref[:, h].reshape(QUERIES, HEAD)
-        scores, values = [], []
-        for kv in (own_ref, far_ref):
-            scores.append(nt(query, kv[0, :, cols]))
-            values.append(kv[1, :, cols])
-        scores[0] = jnp.where(other_rows, scores[0], NEGATIVE)
+        stale, new = nt(query, own_ref[0, :, cols]), nt(query, fresh_ref[h, 1])
+        scores = [jnp.where(other_rows, stale, new), nt(query, far_ref[0, :, cols])]
+        values = [None, far_ref[1, :, cols]]
         for kv in (near_ref, next_ref, mid_ref):
             scores.append(nt(query, kv[:, 0, :, cols].reshape(2 * BLOCK, HEAD)))
             values.append(kv[:, 1, :, cols].reshape(2 * BLOCK, HEAD))
-        scores.append(jnp.where(other_rows, NEGATIVE, nt(query, fresh_ref[h, 1])))
-        values.append(fresh_ref[h, 2])
         scores.append(nt(query, text_ref[0, pl.ds(first, text_rows), cols]))
         values.append(text_ref[1, pl.ds(first, text_rows), cols])
         top = jnp.max(scores[0], axis=-1, keepdims=True)
@@ -119,7 +114,13 @@
         for s, v in zip(scores, values):
             weights = jnp.exp2(s - top)
             total += jnp.sum(weights, axis=-1, keepdims=True)
-            summed += nn(weights.astype(BF16), v)
+            weights = weights.astype(BF16)
+            if v is None:
+                nothing = jnp.zeros_like(weights)
+                summed += nn(jnp.where(other_rows, weights, nothing), own_ref[1, :, cols])
+                summed += nn(jnp.where(other_rows, nothing, weights), fresh_ref[h, 2])
+            else:
+                summed += nn(weights, v)
         summed = (summed / total).astype(BF16)
         pieces = split_level(top + jnp.log2(total))
         for b in range(SHARE):

time: 99.8 us -> 99.3 us (level)
  no operation moved by 1% of the time
where the time goes in v5:
time: 99.3 us; the launch traced here: 98.2 us
  blocking collectives  74 us (75%)
  starting transfers between devices  16.8 us (17%)
  Pallas kernels  5.98 us (6%)
  local copies, waits for them, and re-layouts  1.15 us (1%)
    all_to_all x1, blocking collectives, project(): lax.all_to_all(jnp.broadcast_to(tokens[None], (PARTS, BLOCK, COLS)), 'ten...  16.8 us
    all_to_all x1, blocking collectives, local(): parts = lax.all_to_all(parts, 'tensor', 0, 0)  14.5 us
    all_to_all x1, blocking collectives, local(): message = lax.all_to_all(message, ('guidance', 'za', 'core'), 0, 0)  12.9 us
    all_gather x1, blocking collectives, hand_out(): return (lax.all_gather(fresh[:, 0], ('za', 'core')), fresh)  9.34 us
    all_gather x1, blocking collectives, local(): chip = lax.all_gather(own, 'core')  8.71 us
    ppermute x1, starting transfers between devices, local(): near = lax.ppermute(chip, ('zf', 'core'), by_core(4))  7.07 us
    all_gather x1, blocking collectives, hand_out(): heads = lax.all_gather(away, 'guidance')  6.07 us
    pallas_call x5, Pallas kernels, call(): pl.pallas_call(kernel, out_shape=out_shape, compiler_params=pltpu.Compile...  5.98 us
  transfers between devices with their start and end apart: 4, of which 0 were waited for; matrix products, arithmetic and copies ran while one was open for 1% of the time, Pallas kernels for 2%

profile of v5, /device:TPU:1, one launch (start us, length us, event | category | flops | bytes accessed | tf_op | source)
XLA Modules:
  0.0 98.2 jit_solution(4454458909271240938)
XLA Ops:
  0.0 8.7 %all-gather.2 = bf16[4,1,128,256]{3,2,1,0:T(8,128)(2,1)S(1)} all-gather(bf16[2,1,128,256]{3,2,1,0:T(8,128)(2,1)} %param.14), channel_id=4, replica_groups=mesh['zf'=4,'zb'=2,'za'=2,'core'=2,'tensor'=8,'guidance'=2] {'core'}, dimensions={0}, use_global_device_ids=true | all-gather | bytes 393216 | tf_op jit(solution)/shard_map/all_gather | solution.py:198
  8.7 7.1 %collective-permute-start = (bf16[2,2,128,256]{3,2,1,0:T(8,128)(2,1)S(1)}, bf16[2,2,128,256]{3,2,1,0:T(8,128)(2,1)S(1)}, u32[]{:S(2)}, u32[]{:S(2)}) collective-permute-start(bf16[2,2,128,256]{3,2,1,0:T(8,128)(2,1)S(1)} %bitcast.15), channel_id=1, source_target_pairs={{0,128},{16,400},{128,256},{144,16},{256,384},{272,144},{384,0},{4... | collective-permute-start | bytes 786440 | tf_op jit(solution)/shard_map/ppermute | solution.py:199
  15.8 4.3 %collective-permute-start.1 = (bf16[2,2,128,256]{3,2,1,0:T(8,128)(2,1)S(1)}, bf16[2,2,128,256]{3,2,1,0:T(8,128)(2,1)S(1)}, u32[]{:S(2)}, u32[]{:S(2)}) collective-permute-start(bf16[2,2,128,256]{3,2,1,0:T(8,128)(2,1)S(1)} %bitcast.16), channel_id=1, source_target_pairs={{0,64},{16,464},{64,128},{80,16},{128,192},{144,80},{192,256},{208... | collective-permute-start | bytes 786440 | tf_op jit(solution)/shard_map/ppermute | solution.py:200
  20.1 19.6 %conditional.2 = ((bf16[3,128,128]{2,1,0:T(8,128)(2,1)S(1)}, bf16[3,128,128]{2,1,0:T(8,128)(2,1)S(1)})) conditional(s32[]{:T(128)} %convert_element_type.4, () %tuple.22, (bf16[128,384]{1,0:T(8,128)(2,1)}, f32[3,2,3072]{2,1,0:T(2,128)}, bf16[3,3072,128]{2,1,0:T(8,128)(2,1)}) %tuple.23), branch_computations={%region_0.0_spmd, %region_1.0_spmd} | conditional | bytes 12189760 | solution.py:186
  20.1 0.0 copy-start
  20.1 0.0 copy-start.6
  20.1 1.1 %broadcast_in_dim.0 = bf16[8,128,384]{2,1,0:T(8,128)(2,1)S(1)} broadcast(bf16[128,384]{1,0:T(8,128)(2,1)} %get-tuple-element.15), dimensions={1,2} | broadcast | bytes 884736 | tf_op jit(solution)/shard_map/cond/branch_1_fun/broadcast_in_dim | solution.py:204
  21.2 16.8 %all_to_all.14.x_ref = bf16[8,128,384]{2,1,0:T(8,128)(2,1)S(1)} all-to-all(bf16[8,128,384]{2,1,0:T(8,128)(2,1)S(1)} %broadcast_in_dim.0), channel_id=1, replica_groups=mesh['zf'=4,'zb'=2,'za'=2,'core'=2,'tensor'=8,'guidance'=2] {'tensor'}, dimensions={0} | all-to-all | bytes 1572864 | tf_op jit(solution)/shard_map/cond/branch_1_fun/all_to_all | solution.py:203
  38.0 0.0 copy-done
  38.0 0.0 copy-done.6
  38.0 1.6 %branch_1_fun.1 = (bf16[3,128,128]{2,1,0:T(8,128)(2,1)S(1)}, bf16[3,128,128]{2,1,0:T(8,128)(2,1)S(1)}) custom-call(bf16[8,128,384]{2,1,0:T(8,128)(2,1)S(1)} %all_to_all.14.x_ref, f32[3,2,3072]{2,1,0:T(2,128)S(1)} %copy-done.6, bf16[3,3072,128]{2,1,0:T(8,128)(2,1)S(1)} %copy-done), custom_call_target="tpu_custom_call" | custom-call | tf_op jit(solution)/shard_map/cond/branch_1_fun/pallas_call | solution.py:169
  39.7 0.0 copy-start.2
  39.7 0.0 copy-start.3
  39.7 0.0 collective-permute-done.near_ref
  39.7 0.0 collective-permute-done.1.next_ref
  39.7 2.5 %collective-permute-start.3 = (bf16[2,2,128,256]{3,2,1,0:T(8,128)(2,1)S(1)}, bf16[2,2,128,256]{3,2,1,0:T(8,128)(2,1)S(1)}, u32[]{:S(2)}, u32[]{:S(2)}) collective-permute-start(bf16[2,2,128,256]{3,2,1,0:T(8,128)(2,1)S(1)} %collective-permute-done.near_ref), channel_id=1, source_target_pairs={{0,64},{16,464},{64,128},{80,16},{128,192},{144,80},{192,256},{208... | collective-permute-start | bytes 786440 | tf_op jit(solution)/shard_map/ppermute | solution.py:212
  42.3 2.9 %collective-permute-start.2 = (bf16[2,128,256]{2,1,0:T(8,128)(2,1)S(1)}, bf16[2,128,256]{2,1,0:T(8,128)(2,1)S(1)}, u32[]{:S(2)}, u32[]{:S(2)}) collective-permute-start(bf16[2,128,256]{2,1,0:T(8,128)(2,1)S(1)} %select_bitcast_fusion), channel_id=1, source_target_pairs={{0,128},{16,400},{128,256},{144,16},{256,384},{272,144},{384,0},{4... | collective-permute-start | bytes 393224 | tf_op jit(solution)/shard_map/ppermute | solution.py:213
  45.2 0.0 copy-start.1
  45.2 0.0 copy-start.5
  45.3 15.5 %conditional.3 = (bf16[4,2,128,128]{3,2,1,0:T(8,128)(2,1)S(1)}, bf16[2,3,128,128]{3,2,1,0:T(8,128)(2,1)S(1)}) conditional(s32[]{:T(128)} %convert_element_type.4, () %tuple.21, (bf16[3,128,128]{2,1,0:T(8,128)(2,1)S(1)}, bf16[3,128,128]{2,1,0:T(8,128)(2,1)S(1)}) %tuple.25), branch_computations={%region_2.3_spmd, %region_3.4_spmd} | conditional | flops 229379 | bytes 1769518 | solution.py:186
  45.3 6.1 %all-gather = bf16[6,128,128]{2,1,0:T(8,128)(2,1)S(1)} all-gather(bf16[3,128,128]{2,1,0:T(8,128)(2,1)S(1)} %get-tuple-element.19), channel_id=2, replica_groups=mesh['zf'=4,'zb'=2,'za'=2,'core'=2,'tensor'=8,'guidance'=2] {'guidance'}, dimensions={0}, use_global_device_ids=true | all-gather | bytes 294912 | tf_op jit(solution)/shard_map/cond/branch_1_fun/all_gather | solution.py:216
  51.4 9.3 %all-gather.1 = bf16[8,1,128,128]{3,2,1,0:T(8,128)(2,1)S(1)} all-gather(bf16[2,1,128,128]{3,2,1,0:T(8,128)(2,1)S(1)} %fusion.2), channel_id=3, replica_groups=mesh['zf'=4,'zb'=2,'za'=2,'core'=2,'tensor'=8,'guidance'=2] {'za','core'}, dimensions={0}, use_global_device_ids=true | all-gather | bytes 327680 | tf_op jit(solution)/shard_map/cond/branch_1_fun/all_gather | solution.py:221
  60.7 0.0 collective-permute-done.2.far_ref
  60.8 0.0 collective-permute-done.3.mid_ref
  60.8 0.0 copy-done.2
  60.8 0.0 copy-done.3
  60.8 2.4 %shard_map.65 = bf16[8,144,128]{2,1,0:T(8,128)(2,1)S(1)} custom-call(bf16[4,2,128,128]{3,2,1,0:T(8,128)(2,1)S(1)} %get-tuple-element.30.query_ref, bf16[2,3,128,128]{3,2,1,0:T(8,128)(2,1)S(1)} %get-tuple-element.31.fresh_ref, bf16[2,128,256]{2,1,0:T(8,128)(2,1)S(1)} %bitcast.12, bf16[2,128,256]{2,1,0:T(8,128)(2,1)S(1)} %collective-permute-done.2.far_ref, ...), custom_call_target="tpu_custom_call" | custom-call | tf_op jit(solution)/shard_map/pallas_call | solution.py:169
  63.2 12.9 %all_to_all.15.reply_ref = bf16[8,144,128]{2,1,0:T(8,128)(2,1)S(1)} all-to-all(bf16[8,144,128]{2,1,0:T(8,128)(2,1)S(1)} %shard_map.65), channel_id=1, replica_groups=mesh['zf'=4,'zb'=2,'za'=2,'core'=2,'tensor'=8,'guidance'=2] {'guidance',..., dimensions={0} | all-to-all | bytes 589824 | tf_op jit(solution)/shard_map/all_to_all | solution.py:227
  76.0 0.0 copy-done.1
  76.0 0.0 copy-done.5
  76.0 0.0 copy-start.4
  76.0 1.2 %shard_map.66 = bf16[8,128,384]{2,1,0:T(8,128)(2,1)S(1)} custom-call(bf16[8,144,128]{2,1,0:T(8,128)(2,1)S(1)} %all_to_all.15.reply_ref, f32[3,2,3072]{2,1,0:T(2,128)S(1)} %copy-done.5, bf16[128,3072]{1,0:T(8,128)(2,1)S(1)} %copy-done.1), custom_call_target="tpu_custom_call" | custom-call | tf_op jit(solution)/shard_map/pallas_call | solution.py:169
  77.2 14.5 %all_to_all.16.parts_ref = bf16[8,128,384]{2,1,0:T(8,128)(2,1)S(1)} all-to-all(bf16[8,128,384]{2,1,0:T(8,128)(2,1)S(1)} %shard_map.66), channel_id=1, replica_groups=mesh['zf'=4,'zb'=2,'za'=2,'core'=2,'tensor'=8,'guidance'=2] {'tensor'}, dimensions={0} | all-to-all | bytes 1572864 | tf_op jit(solution)/shard_map/all_to_all | solution.py:229
  91.7 0.1 shard_map.67
  91.8 5.6 %all-gather.3 = bf16[256,384]{1,0:T(8,128)(2,1)S(1)} all-gather(bf16[128,384]{1,0:T(8,128)(2,1)S(1)} %shard_map.67), channel_id=5, replica_groups=mesh['zf'=4,'zb'=2,'za'=2,'core'=2,'tensor'=8,'guidance'=2] {'guidance'}, dimensions={0}, use_global_device_ids=true | all-gather | bytes 294912 | tf_op jit(solution)/shard_map/all_gather | solution.py:230
  97.5 0.0 copy-done.4
  97.5 0.7 shard_map.68
  (4 shorter events, 0.1 us)
Async XLA Ops:
  8.7 31.0 %collective-permute-start = (bf16[2,2,128,256]{3,2,1,0:T(8,128)(2,1)S(1)}, bf16[2,2,128,256]{3,2,1,0:T(8,128)(2,1)S(1)}, u32[]{:S(2)}, u32[]{:S(2)}) collective-permute-start(bf16[2,2,128,256]{3,2,1,0:T(8,128)(2,1)S(1)} %bitcast.15), channel_id=1, source_target_pairs={{0,128},{16,400},{128,256},{144,16},{256,384},{272,144},{384,0},{4... | collective-permute-start | bytes 786440 | tf_op jit(solution)/shard_map/ppermute | solution.py:199
  15.8 23.9 %collective-permute-start.1 = (bf16[2,2,128,256]{3,2,1,0:T(8,128)(2,1)S(1)}, bf16[2,2,128,256]{3,2,1,0:T(8,128)(2,1)S(1)}, u32[]{:S(2)}, u32[]{:S(2)}) collective-permute-start(bf16[2,2,128,256]{3,2,1,0:T(8,128)(2,1)S(1)} %bitcast.16), channel_id=1, source_target_pairs={{0,64},{16,464},{64,128},{80,16},{128,192},{144,80},{192,256},{208... | collective-permute-start | bytes 786440 | tf_op jit(solution)/shard_map/ppermute | solution.py:200
  20.1 17.9 %copy-start = (bf16[3,3072,128]{2,1,0:T(8,128)(2,1)S(1)}, bf16[3,3072,128]{2,1,0:T(8,128)(2,1)}, u32[]{:S(2)}) copy-start(bf16[3,3072,128]{2,1,0:T(8,128)(2,1)} %get-tuple-element.35.w_ref) | copy-start | bytes 7077892 | tf_op jit(solution)/shard_map/cond
  20.1 17.9 %copy-start.6 = (f32[3,2,3072]{2,1,0:T(2,128)S(1)}, f32[3,2,3072]{2,1,0:T(2,128)}, u32[]{:S(2)}) copy-start(f32[3,2,3072]{2,1,0:T(2,128)} %get-tuple-element.16.mod_ref) | copy-start | bytes 221188 | tf_op jit(solution)/shard_map/cond
  39.7 21.1 %copy-start.2 = (bf16[2,1,128,256]{3,2,1,0:T(8,128)(2,1)S(1)}, bf16[2,1,128,256]{3,2,1,0:T(8,128)(2,1)}, u32[]{:S(2)}) copy-start(bf16[2,1,128,256]{3,2,1,0:T(8,128)(2,1)} %param.14) | copy-start | bytes 393220
  39.7 21.1 %copy-start.3 = (bf16[2,1,256,256]{3,2,1,0:T(8,128)(2,1)S(1)}, bf16[2,1,256,256]{3,2,1,0:T(8,128)(2,1)}, u32[]{:S(2)}) copy-start(bf16[2,1,256,256]{3,2,1,0:T(8,128)(2,1)} %param.15) | copy-start | bytes 786436
  39.7 21.0 %collective-permute-start.3 = (bf16[2,2,128,256]{3,2,1,0:T(8,128)(2,1)S(1)}, bf16[2,2,128,256]{3,2,1,0:T(8,128)(2,1)S(1)}, u32[]{:S(2)}, u32[]{:S(2)}) collective-permute-start(bf16[2,2,128,256]{3,2,1,0:T(8,128)(2,1)S(1)} %collective-permute-done.near_ref), channel_id=1, source_target_pairs={{0,64},{16,464},{64,128},{80,16},{128,192},{144,80},{192,256},{208... | collective-permute-start | bytes 786440 | tf_op jit(solution)/shard_map/ppermute | solution.py:212
  42.3 18.4 %collective-permute-start.2 = (bf16[2,128,256]{2,1,0:T(8,128)(2,1)S(1)}, bf16[2,128,256]{2,1,0:T(8,128)(2,1)S(1)}, u32[]{:S(2)}, u32[]{:S(2)}) collective-permute-start(bf16[2,128,256]{2,1,0:T(8,128)(2,1)S(1)} %select_bitcast_fusion), channel_id=1, source_target_pairs={{0,128},{16,400},{128,256},{144,16},{256,384},{272,144},{384,0},{4... | collective-permute-start | bytes 393224 | tf_op jit(solution)/shard_map/ppermute | solution.py:213
  45.2 30.8 %copy-start.1 = (bf16[128,3072]{1,0:T(8,128)(2,1)S(1)}, bf16[128,3072]{1,0:T(8,128)(2,1)}, u32[]{:S(2)}) copy-start(bf16[128,3072]{1,0:T(8,128)(2,1)} %w_ref.1) | copy-start | bytes 2359300
  45.2 30.8 %copy-start.5 = (f32[3,2,3072]{2,1,0:T(2,128)S(1)}, f32[3,2,3072]{2,1,0:T(2,128)}, u32[]{:S(2)}) copy-start(f32[3,2,3072]{2,1,0:T(2,128)} %mod_ref.1) | copy-start | bytes 221188
  76.0 21.5 %copy-start.4 = (bf16[128,384]{1,0:T(8,128)(2,1)S(1)}, bf16[128,384]{1,0:T(8,128)(2,1)}, u32[]{:S(2)}) copy-start(bf16[128,384]{1,0:T(8,128)(2,1)} %tokens_ref.1) | copy-start | bytes 294916

commit v6 on v5

--- a/solution.py
+++ b/solution.py
@@ -106,14 +106,22 @@
             values.append(kv[:, 1, :, cols].reshape(2 * BLOCK, HEAD))
         scores.append(nt(query, text_ref[0, pl.ds(first, text_rows), cols]))
         values.append(text_ref[1, pl.ds(first, text_rows), cols])
-        top = jnp.max(scores[0], axis=-1, keepdims=True)
-        for s in scores[1:]:
-            top = jnp.maximum(top, jnp.max(s, axis=-1, keepdims=True))
+        wide = scores[0]
+        for s in scores[1:-1]:
+            for i in range(0, s.shape[1], HEAD):
+                wide = jnp.maximum(wide, s[:, i : i + HEAD])
+        top = jnp.max(wide, axis=-1, keepdims=True)
+        top = jnp.maximum(top, jnp.max(scores[-1], axis=-1, keepdims=True))
+        wide = jnp.zeros((QUERIES, HEAD), F32)
         total = jnp.zeros((QUERIES, 1), F32)
         summed = jnp.zeros((QUERIES, HEAD), F32)
         for s, v in zip(scores, values):
             weights = jnp.exp2(s - top)
-            total += jnp.sum(weights, axis=-1, keepdims=True)
+            if s.shape[1] % HEAD:
+                total += jnp.sum(weights, axis=-1, keepdims=True)
+            else:
+                for i in range(0, s.shape[1], HEAD):
+                    wide += weights[:, i : i + HEAD]
             weights = weights.astype(BF16)
             if v is None:
                 nothing = jnp.zeros_like(weights)
@@ -121,6 +129,7 @@
                 summed += nn(jnp.where(other_rows, nothing, weights), fresh_ref[h, 2])
             else:
                 summed += nn(weights, v)
+        total += jnp.sum(wide, axis=-1, keepdims=True)
         summed = (summed / total).astype(BF16)
         pieces = split_level(top + jnp.log2(total))
         for b in range(SHARE):
@@ -210,7 +219,7 @@
     own_pass, away = together(project, tokens, modulation, w_qkv)
     away, near, beside = lax.optimization_barrier((away, near, beside))
     mid = lax.ppermute(near, ("zf", "zb", "core"), by_core(8))
-    far = lax.ppermute(jnp.where(core == 0, near[0], near[1]), ("zf", "core"), by_core(4))
+    far = lax.ppermute(lax.dynamic_index_in_dim(near, core, 0, keepdims=False), ("zf", "core"), by_core(4))
 
     def hand_out(own_pass, away):
         heads = lax.all_gather(away, "guidance")

time: 99.3 us -> 99.3 us (level)
  no operation moved by 1% of the time
where the time goes in v6:
time: 99.3 us; the launch traced here: 98.2 us
  blocking collectives  74 us (75%)
  starting transfers between devices  16.8 us (17%)
  Pallas kernels  5.89 us (6%)
  local copies, waits for them, and re-layouts  1.17 us (1%)
    all_to_all x1, blocking collectives, project(): lax.all_to_all(jnp.broadcast_to(tokens[None], (PARTS, BLOCK, COLS)), 'ten...  16.8 us
    all_to_all x1, blocking collectives, local(): parts = lax.all_to_all(parts, 'tensor', 0, 0)  14.5 us
    all_to_all x1, blocking collectives, local(): message = lax.all_to_all(message, ('guidance', 'za', 'core'), 0, 0)  12.9 us
    all_gather x1, blocking collectives, hand_out(): return (lax.all_gather(fresh[:, 0], ('za', 'core')), fresh)  9.34 us
    all_gather x1, blocking collectives, local(): chip = lax.all_gather(own, 'core')  8.71 us
    ppermute x1, starting transfers between devices, local(): near = lax.ppermute(chip, ('zf', 'core'), by_core(4))  7.07 us
    all_gather x1, blocking collectives, hand_out(): heads = lax.all_gather(away, 'guidance')  6.07 us
    pallas_call x5, Pallas kernels, call(): pl.pallas_call(kernel, out_shape=out_shape, compiler_params=pltpu.Compile...  5.89 us
  transfers between devices with their start and end apart: 4, of which 0 were waited for; matrix products, arithmetic and copies ran while one was open for 1% of the time, Pallas kernels for 2%

profile of v6, /device:TPU:1, one launch (start us, length us, event | category | flops | bytes accessed | tf_op | source)
XLA Modules:
  0.0 98.2 jit_solution(1972598863897451051)
XLA Ops:
  0.0 8.7 %all-gather.2 = bf16[4,1,128,256]{3,2,1,0:T(8,128)(2,1)S(1)} all-gather(bf16[2,1,128,256]{3,2,1,0:T(8,128)(2,1)} %param.14), channel_id=4, replica_groups=mesh['zf'=4,'zb'=2,'za'=2,'core'=2,'tensor'=8,'guidance'=2] {'core'}, dimensions={0}, use_global_device_ids=true | all-gather | bytes 393216 | tf_op jit(solution)/shard_map/all_gather | solution.py:207
  8.7 7.1 %collective-permute-start = (bf16[2,2,128,256]{3,2,1,0:T(8,128)(2,1)S(1)}, bf16[2,2,128,256]{3,2,1,0:T(8,128)(2,1)S(1)}, u32[]{:S(2)}, u32[]{:S(2)}) collective-permute-start(bf16[2,2,128,256]{3,2,1,0:T(8,128)(2,1)S(1)} %bitcast.15), channel_id=1, source_target_pairs={{0,128},{16,400},{128,256},{144,16},{256,384},{272,144},{384,0},{4... | collective-permute-start | bytes 786440 | tf_op jit(solution)/shard_map/ppermute | solution.py:208
  15.8 4.3 %collective-permute-start.1 = (bf16[2,2,128,256]{3,2,1,0:T(8,128)(2,1)S(1)}, bf16[2,2,128,256]{3,2,1,0:T(8,128)(2,1)S(1)}, u32[]{:S(2)}, u32[]{:S(2)}) collective-permute-start(bf16[2,2,128,256]{3,2,1,0:T(8,128)(2,1)S(1)} %bitcast.16), channel_id=1, source_target_pairs={{0,64},{16,464},{64,128},{80,16},{128,192},{144,80},{192,256},{208... | collective-permute-start | bytes 786440 | tf_op jit(solution)/shard_map/ppermute | solution.py:209
  20.1 19.6 %conditional.2 = ((bf16[3,128,128]{2,1,0:T(8,128)(2,1)S(1)}, bf16[3,128,128]{2,1,0:T(8,128)(2,1)S(1)})) conditional(s32[]{:T(128)} %convert_element_type.4, () %tuple.22, (bf16[128,384]{1,0:T(8,128)(2,1)}, f32[3,2,3072]{2,1,0:T(2,128)}, bf16[3,3072,128]{2,1,0:T(8,128)(2,1)}) %tuple.23), branch_computations={%region_0.0_spmd, %region_1.0_spmd} | conditional | bytes 12189760 | solution.py:195
  20.1 0.0 copy-start
  20.1 0.0 copy-start.6
  20.1 1.1 %broadcast_in_dim.0 = bf16[8,128,384]{2,1,0:T(8,128)(2,1)S(1)} broadcast(bf16[128,384]{1,0:T(8,128)(2,1)} %get-tuple-element.15), dimensions={1,2} | broadcast | bytes 884736 | tf_op jit(solution)/shard_map/cond/branch_1_fun/broadcast_in_dim | solution.py:213
  21.2 16.8 %all_to_all.14.x_ref = bf16[8,128,384]{2,1,0:T(8,128)(2,1)S(1)} all-to-all(bf16[8,128,384]{2,1,0:T(8,128)(2,1)S(1)} %broadcast_in_dim.0), channel_id=1, replica_groups=mesh['zf'=4,'zb'=2,'za'=2,'core'=2,'tensor'=8,'guidance'=2] {'tensor'}, dimensions={0} | all-to-all | bytes 1572864 | tf_op jit(solution)/shard_map/cond/branch_1_fun/all_to_all | solution.py:212
  38.0 0.0 copy-done
  38.0 0.0 copy-done.6
  38.0 1.6 %branch_1_fun.1 = (bf16[3,128,128]{2,1,0:T(8,128)(2,1)S(1)}, bf16[3,128,128]{2,1,0:T(8,128)(2,1)S(1)}) custom-call(bf16[8,128,384]{2,1,0:T(8,128)(2,1)S(1)} %all_to_all.14.x_ref, f32[3,2,3072]{2,1,0:T(2,128)S(1)} %copy-done.6, bf16[3,3072,128]{2,1,0:T(8,128)(2,1)S(1)} %copy-done), custom_call_target="tpu_custom_call" | custom-call | tf_op jit(solution)/shard_map/cond/branch_1_fun/pallas_call | solution.py:178
  39.7 0.0 copy-start.2
  39.7 0.0 copy-start.3
  39.7 0.0 collective-permute-done.near_ref
  39.7 0.0 collective-permute-done.1.next_ref
  39.7 2.5 %collective-permute-start.3 = (bf16[2,2,128,256]{3,2,1,0:T(8,128)(2,1)S(1)}, bf16[2,2,128,256]{3,2,1,0:T(8,128)(2,1)S(1)}, u32[]{:S(2)}, u32[]{:S(2)}) collective-permute-start(bf16[2,2,128,256]{3,2,1,0:T(8,128)(2,1)S(1)} %collective-permute-done.near_ref), channel_id=1, source_target_pairs={{0,64},{16,464},{64,128},{80,16},{128,192},{144,80},{192,256},{208... | collective-permute-start | bytes 786440 | tf_op jit(solution)/shard_map/ppermute | solution.py:221
  42.3 2.9 %collective-permute-start.2 = (bf16[2,128,256]{2,1,0:T(8,128)(2,1)S(1)}, bf16[2,128,256]{2,1,0:T(8,128)(2,1)S(1)}, u32[]{:S(2)}, u32[]{:S(2)}) collective-permute-start(bf16[2,128,256]{2,1,0:T(8,128)(2,1)S(1)} %dynamic-slice_bitcast_fusion), channel_id=1, source_target_pairs={{0,128},{16,400},{128,256},{144,16},{256,384},{272,144},{384,0},{4... | collective-permute-start | bytes 393224 | tf_op jit(solution)/shard_map/ppermute | solution.py:222
  45.2 0.0 copy-start.1
  45.2 0.0 copy-start.5
  45.2 15.5 %conditional.3 = (bf16[4,2,128,128]{3,2,1,0:T(8,128)(2,1)S(1)}, bf16[2,3,128,128]{3,2,1,0:T(8,128)(2,1)S(1)}) conditional(s32[]{:T(128)} %convert_element_type.4, () %tuple.21, (bf16[3,128,128]{2,1,0:T(8,128)(2,1)S(1)}, bf16[3,128,128]{2,1,0:T(8,128)(2,1)S(1)}) %tuple.25), branch_computations={%region_2.3_spmd, %region_3.4_spmd} | conditional | flops 229379 | bytes 1769518 | solution.py:195
  45.3 6.1 %all-gather = bf16[6,128,128]{2,1,0:T(8,128)(2,1)S(1)} all-gather(bf16[3,128,128]{2,1,0:T(8,128)(2,1)S(1)} %get-tuple-element.19), channel_id=2, replica_groups=mesh['zf'=4,'zb'=2,'za'=2,'core'=2,'tensor'=8,'guidance'=2] {'guidance'}, dimensions={0}, use_global_device_ids=true | all-gather | bytes 294912 | tf_op jit(solution)/shard_map/cond/branch_1_fun/all_gather | solution.py:225
  51.4 9.3 %all-gather.1 = bf16[8,1,128,128]{3,2,1,0:T(8,128)(2,1)S(1)} all-gather(bf16[2,1,128,128]{3,2,1,0:T(8,128)(2,1)S(1)} %fusion.2), channel_id=3, replica_groups=mesh['zf'=4,'zb'=2,'za'=2,'core'=2,'tensor'=8,'guidance'=2] {'za','core'}, dimensions={0}, use_global_device_ids=true | all-gather | bytes 327680 | tf_op jit(solution)/shard_map/cond/branch_1_fun/all_gather | solution.py:230
  60.7 0.0 collective-permute-done.2.far_ref
  60.7 0.0 collective-permute-done.3.mid_ref
  60.8 0.0 copy-done.2
  60.8 0.0 copy-done.3
  60.8 2.3 %shard_map.65 = bf16[8,144,128]{2,1,0:T(8,128)(2,1)S(1)} custom-call(bf16[4,2,128,128]{3,2,1,0:T(8,128)(2,1)S(1)} %get-tuple-element.30.query_ref, bf16[2,3,128,128]{3,2,1,0:T(8,128)(2,1)S(1)} %get-tuple-element.31.fresh_ref, bf16[2,128,256]{2,1,0:T(8,128)(2,1)S(1)} %bitcast.12, bf16[2,128,256]{2,1,0:T(8,128)(2,1)S(1)} %collective-permute-done.2.far_ref, ...), custom_call_target="tpu_custom_call" | custom-call | tf_op jit(solution)/shard_map/pallas_call | solution.py:178
  63.1 12.9 %all_to_all.15.reply_ref = bf16[8,144,128]{2,1,0:T(8,128)(2,1)S(1)} all-to-all(bf16[8,144,128]{2,1,0:T(8,128)(2,1)S(1)} %shard_map.65), channel_id=1, replica_groups=mesh['zf'=4,'zb'=2,'za'=2,'core'=2,'tensor'=8,'guidance'=2] {'guidance',..., dimensions={0} | all-to-all | bytes 589824 | tf_op jit(solution)/shard_map/all_to_all | solution.py:236
  76.0 0.0 copy-done.1
  76.0 0.0 copy-done.5
  76.0 0.0 copy-start.4
  76.0 1.2 %shard_map.66 = bf16[8,128,384]{2,1,0:T(8,128)(2,1)S(1)} custom-call(bf16[8,144,128]{2,1,0:T(8,128)(2,1)S(1)} %all_to_all.15.reply_ref, f32[3,2,3072]{2,1,0:T(2,128)S(1)} %copy-done.5, bf16[128,3072]{1,0:T(8,128)(2,1)S(1)} %copy-done.1), custom_call_target="tpu_custom_call" | custom-call | tf_op jit(solution)/shard_map/pallas_call | solution.py:178
  77.2 14.5 %all_to_all.16.parts_ref = bf16[8,128,384]{2,1,0:T(8,128)(2,1)S(1)} all-to-all(bf16[8,128,384]{2,1,0:T(8,128)(2,1)S(1)} %shard_map.66), channel_id=1, replica_groups=mesh['zf'=4,'zb'=2,'za'=2,'core'=2,'tensor'=8,'guidance'=2] {'tensor'}, dimensions={0} | all-to-all | bytes 1572864 | tf_op jit(solution)/shard_map/all_to_all | solution.py:238
  91.7 0.1 shard_map.67
  91.8 5.6 %all-gather.3 = bf16[256,384]{1,0:T(8,128)(2,1)S(1)} all-gather(bf16[128,384]{1,0:T(8,128)(2,1)S(1)} %shard_map.67), channel_id=5, replica_groups=mesh['zf'=4,'zb'=2,'za'=2,'core'=2,'tensor'=8,'guidance'=2] {'guidance'}, dimensions={0}, use_global_device_ids=true | all-gather | bytes 294912 | tf_op jit(solution)/shard_map/all_gather | solution.py:239
  97.5 0.0 copy-done.4
  97.5 0.7 shard_map.68
  (4 shorter events, 0.1 us)
Async XLA Ops:
  8.7 31.0 %collective-permute-start = (bf16[2,2,128,256]{3,2,1,0:T(8,128)(2,1)S(1)}, bf16[2,2,128,256]{3,2,1,0:T(8,128)(2,1)S(1)}, u32[]{:S(2)}, u32[]{:S(2)}) collective-permute-start(bf16[2,2,128,256]{3,2,1,0:T(8,128)(2,1)S(1)} %bitcast.15), channel_id=1, source_target_pairs={{0,128},{16,400},{128,256},{144,16},{256,384},{272,144},{384,0},{4... | collective-permute-start | bytes 786440 | tf_op jit(solution)/shard_map/ppermute | solution.py:208
  15.8 23.9 %collective-permute-start.1 = (bf16[2,2,128,256]{3,2,1,0:T(8,128)(2,1)S(1)}, bf16[2,2,128,256]{3,2,1,0:T(8,128)(2,1)S(1)}, u32[]{:S(2)}, u32[]{:S(2)}) collective-permute-start(bf16[2,2,128,256]{3,2,1,0:T(8,128)(2,1)S(1)} %bitcast.16), channel_id=1, source_target_pairs={{0,64},{16,464},{64,128},{80,16},{128,192},{144,80},{192,256},{208... | collective-permute-start | bytes 786440 | tf_op jit(solution)/shard_map/ppermute | solution.py:209
  20.1 17.9 %copy-start = (bf16[3,3072,128]{2,1,0:T(8,128)(2,1)S(1)}, bf16[3,3072,128]{2,1,0:T(8,128)(2,1)}, u32[]{:S(2)}) copy-start(bf16[3,3072,128]{2,1,0:T(8,128)(2,1)} %get-tuple-element.35.w_ref) | copy-start | bytes 7077892 | tf_op jit(solution)/shard_map/cond
  20.1 17.9 %copy-start.6 = (f32[3,2,3072]{2,1,0:T(2,128)S(1)}, f32[3,2,3072]{2,1,0:T(2,128)}, u32[]{:S(2)}) copy-start(f32[3,2,3072]{2,1,0:T(2,128)} %get-tuple-element.16.mod_ref) | copy-start | bytes 221188 | tf_op jit(solution)/shard_map/cond
  39.7 21.1 %copy-start.2 = (bf16[2,1,128,256]{3,2,1,0:T(8,128)(2,1)S(1)}, bf16[2,1,128,256]{3,2,1,0:T(8,128)(2,1)}, u32[]{:S(2)}) copy-start(bf16[2,1,128,256]{3,2,1,0:T(8,128)(2,1)} %param.14) | copy-start | bytes 393220
  39.7 21.1 %copy-start.3 = (bf16[2,1,256,256]{3,2,1,0:T(8,128)(2,1)S(1)}, bf16[2,1,256,256]{3,2,1,0:T(8,128)(2,1)}, u32[]{:S(2)}) copy-start(bf16[2,1,256,256]{3,2,1,0:T(8,128)(2,1)} %param.15) | copy-start | bytes 786436
  39.7 21.0 %collective-permute-start.3 = (bf16[2,2,128,256]{3,2,1,0:T(8,128)(2,1)S(1)}, bf16[2,2,128,256]{3,2,1,0:T(8,128)(2,1)S(1)}, u32[]{:S(2)}, u32[]{:S(2)}) collective-permute-start(bf16[2,2,128,256]{3,2,1,0:T(8,128)(2,1)S(1)} %collective-permute-done.near_ref), channel_id=1, source_target_pairs={{0,64},{16,464},{64,128},{80,16},{128,192},{144,80},{192,256},{208... | collective-permute-start | bytes 786440 | tf_op jit(solution)/shard_map/ppermute | solution.py:221
  42.3 18.4 %collective-permute-start.2 = (bf16[2,128,256]{2,1,0:T(8,128)(2,1)S(1)}, bf16[2,128,256]{2,1,0:T(8,128)(2,1)S(1)}, u32[]{:S(2)}, u32[]{:S(2)}) collective-permute-start(bf16[2,128,256]{2,1,0:T(8,128)(2,1)S(1)} %dynamic-slice_bitcast_fusion), channel_id=1, source_target_pairs={{0,128},{16,400},{128,256},{144,16},{256,384},{272,144},{384,0},{4... | collective-permute-start | bytes 393224 | tf_op jit(solution)/shard_map/ppermute | solution.py:222
  45.2 30.8 %copy-start.1 = (bf16[128,3072]{1,0:T(8,128)(2,1)S(1)}, bf16[128,3072]{1,0:T(8,128)(2,1)}, u32[]{:S(2)}) copy-start(bf16[128,3072]{1,0:T(8,128)(2,1)} %w_ref.1) | copy-start | bytes 2359300
  45.2 30.8 %copy-start.5 = (f32[3,2,3072]{2,1,0:T(2,128)S(1)}, f32[3,2,3072]{2,1,0:T(2,128)}, u32[]{:S(2)}) copy-start(f32[3,2,3072]{2,1,0:T(2,128)} %mod_ref.1) | copy-start | bytes 221188
  76.0 21.5 %copy-start.4 = (bf16[128,384]{1,0:T(8,128)(2,1)S(1)}, bf16[128,384]{1,0:T(8,128)(2,1)}, u32[]{:S(2)}) copy-start(bf16[128,384]{1,0:T(8,128)(2,1)} %tokens_ref.1) | copy-start | bytes 294916

commit v7 on v6

--- a/solution.py
+++ b/solution.py
@@ -84,7 +84,7 @@
         top = jnp.maximum(top, level)
     shares = [jnp.exp2(level - top) for level in levels]
     joined = sum(share * part.astype(F32) for share, part in zip(shares, parts))
-    return joined / sum(shares)
+    return joined * (1.0 / sum(shares))
 
 
 def attend_kernel(query_ref, fresh_ref, own_ref, far_ref, near_ref, next_ref, mid_ref, text_ref, out_ref):
@@ -130,7 +130,7 @@
             else:
                 summed += nn(weights, v)
         total += jnp.sum(wide, axis=-1, keepdims=True)
-        summed = (summed / total).astype(BF16)
+        summed = (summed * (1.0 / total)).astype(BF16)
         pieces = split_level(top + jnp.log2(total))
         for b in range(SHARE):
             rows = slice(b * BLOCK, (b + 1) * BLOCK)

time: 99.3 us -> 99.3 us (level)
  no operation moved by 1% of the time
where the time goes in v7:
time: 99.3 us; the launch traced here: 98.2 us
  blocking collectives  74 us (75%)
  starting transfers between devices  16.8 us (17%)
  Pallas kernels  5.9 us (6%)
  local copies, waits for them, and re-layouts  1.17 us (1%)
    all_to_all x1, blocking collectives, project(): lax.all_to_all(jnp.broadcast_to(tokens[None], (PARTS, BLOCK, COLS)), 'ten...  16.8 us
    all_to_all x1, blocking collectives, local(): parts = lax.all_to_all(parts, 'tensor', 0, 0)  14.5 us
    all_to_all x1, blocking collectives, local(): message = lax.all_to_all(message, ('guidance', 'za', 'core'), 0, 0)  12.9 us
    all_gather x1, blocking collectives, hand_out(): return (lax.all_gather(fresh[:, 0], ('za', 'core')), fresh)  9.34 us
    all_gather x1, blocking collectives, local(): chip = lax.all_gather(own, 'core')  8.71 us
    ppermute x1, starting transfers between devices, local(): near = lax.ppermute(chip, ('zf', 'core'), by_core(4))  7.07 us
    all_gather x1, blocking collectives, hand_out(): heads = lax.all_gather(away, 'guidance')  6.07 us
    pallas_call x5, Pallas kernels, call(): pl.pallas_call(kernel, out_shape=out_shape, compiler_params=pltpu.Compile...  5.9 us
  transfers between devices with their start and end apart: 4, of which 0 were waited for; matrix products, arithmetic and copies ran while one was open for 1% of the time, Pallas kernels for 2%

profile of v7, /device:TPU:1, one launch (start us, length us, event | category | flops | bytes accessed | tf_op | source)
XLA Modules:
  0.0 98.2 jit_solution(16750142556961346391)
XLA Ops:
  0.0 8.7 %all-gather.2 = bf16[4,1,128,256]{3,2,1,0:T(8,128)(2,1)S(1)} all-gather(bf16[2,1,128,256]{3,2,1,0:T(8,128)(2,1)} %param.14), channel_id=4, replica_groups=mesh['zf'=4,'zb'=2,'za'=2,'core'=2,'tensor'=8,'guidance'=2] {'core'}, dimensions={0}, use_global_device_ids=true | all-gather | bytes 393216 | tf_op jit(solution)/shard_map/all_gather | solution.py:207
  8.7 7.1 %collective-permute-start = (bf16[2,2,128,256]{3,2,1,0:T(8,128)(2,1)S(1)}, bf16[2,2,128,256]{3,2,1,0:T(8,128)(2,1)S(1)}, u32[]{:S(2)}, u32[]{:S(2)}) collective-permute-start(bf16[2,2,128,256]{3,2,1,0:T(8,128)(2,1)S(1)} %bitcast.15), channel_id=1, source_target_pairs={{0,128},{16,400},{128,256},{144,16},{256,384},{272,144},{384,0},{4... | collective-permute-start | bytes 786440 | tf_op jit(solution)/shard_map/ppermute | solution.py:208
  15.8 4.3 %collective-permute-start.1 = (bf16[2,2,128,256]{3,2,1,0:T(8,128)(2,1)S(1)}, bf16[2,2,128,256]{3,2,1,0:T(8,128)(2,1)S(1)}, u32[]{:S(2)}, u32[]{:S(2)}) collective-permute-start(bf16[2,2,128,256]{3,2,1,0:T(8,128)(2,1)S(1)} %bitcast.16), channel_id=1, source_target_pairs={{0,64},{16,464},{64,128},{80,16},{128,192},{144,80},{192,256},{208... | collective-permute-start | bytes 786440 | tf_op jit(solution)/shard_map/ppermute | solution.py:209
  20.1 19.6 %conditional.2 = ((bf16[3,128,128]{2,1,0:T(8,128)(2,1)S(1)}, bf16[3,128,128]{2,1,0:T(8,128)(2,1)S(1)})) conditional(s32[]{:T(128)} %convert_element_type.4, () %tuple.22, (bf16[128,384]{1,0:T(8,128)(2,1)}, f32[3,2,3072]{2,1,0:T(2,128)}, bf16[3,3072,128]{2,1,0:T(8,128)(2,1)}) %tuple.23), branch_computations={%region_0.0_spmd, %region_1.0_spmd} | conditional | bytes 12189760 | solution.py:195
  20.1 0.0 copy-start
  20.1 0.0 copy-start.6
  20.1 1.1 %broadcast_in_dim.0 = bf16[8,128,384]{2,1,0:T(8,128)(2,1)S(1)} broadcast(bf16[128,384]{1,0:T(8,128)(2,1)} %get-tuple-element.15), dimensions={1,2} | broadcast | bytes 884736 | tf_op jit(solution)/shard_map/cond/branch_1_fun/broadcast_in_dim | solution.py:213
  21.2 16.8 %all_to_all.14.x_ref = bf16[8,128,384]{2,1,0:T(8,128)(2,1)S(1)} all-to-all(bf16[8,128,384]{2,1,0:T(8,128)(2,1)S(1)} %broadcast_in_dim.0), channel_id=1, replica_groups=mesh['zf'=4,'zb'=2,'za'=2,'core'=2,'tensor'=8,'guidance'=2] {'tensor'}, dimensions={0} | all-to-all | bytes 1572864 | tf_op jit(solution)/shard_map/cond/branch_1_fun/all_to_all | solution.py:212
  38.0 0.0 copy-done
  38.0 0.0 copy-done.6
  38.0 1.6 %branch_1_fun.1 = (bf16[3,128,128]{2,1,0:T(8,128)(2,1)S(1)}, bf16[3,128,128]{2,1,0:T(8,128)(2,1)S(1)}) custom-call(bf16[8,128,384]{2,1,0:T(8,128)(2,1)S(1)} %all_to_all.14.x_ref, f32[3,2,3072]{2,1,0:T(2,128)S(1)} %copy-done.6, bf16[3,3072,128]{2,1,0:T(8,128)(2,1)S(1)} %copy-done), custom_call_target="tpu_custom_call" | custom-call | tf_op jit(solution)/shard_map/cond/branch_1_fun/pallas_call | solution.py:178
  39.7 0.0 copy-start.2
  39.7 0.0 copy-start.3
  39.7 0.0 collective-permute-done.near_ref
  39.7 0.0 collective-permute-done.1.next_ref
  39.7 2.5 %collective-permute-start.3 = (bf16[2,2,128,256]{3,2,1,0:T(8,128)(2,1)S(1)}, bf16[2,2,128,256]{3,2,1,0:T(8,128)(2,1)S(1)}, u32[]{:S(2)}, u32[]{:S(2)}) collective-permute-start(bf16[2,2,128,256]{3,2,1,0:T(8,128)(2,1)S(1)} %collective-permute-done.near_ref), channel_id=1, source_target_pairs={{0,64},{16,464},{64,128},{80,16},{128,192},{144,80},{192,256},{208... | collective-permute-start | bytes 786440 | tf_op jit(solution)/shard_map/ppermute | solution.py:221
  42.3 2.9 %collective-permute-start.2 = (bf16[2,128,256]{2,1,0:T(8,128)(2,1)S(1)}, bf16[2,128,256]{2,1,0:T(8,128)(2,1)S(1)}, u32[]{:S(2)}, u32[]{:S(2)}) collective-permute-start(bf16[2,128,256]{2,1,0:T(8,128)(2,1)S(1)} %dynamic-slice_bitcast_fusion), channel_id=1, source_target_pairs={{0,128},{16,400},{128,256},{144,16},{256,384},{272,144},{384,0},{4... | collective-permute-start | bytes 393224 | tf_op jit(solution)/shard_map/ppermute | solution.py:222
  45.2 0.0 copy-start.1
  45.2 0.0 copy-start.5
  45.2 15.5 %conditional.3 = (bf16[4,2,128,128]{3,2,1,0:T(8,128)(2,1)S(1)}, bf16[2,3,128,128]{3,2,1,0:T(8,128)(2,1)S(1)}) conditional(s32[]{:T(128)} %convert_element_type.4, () %tuple.21, (bf16[3,128,128]{2,1,0:T(8,128)(2,1)S(1)}, bf16[3,128,128]{2,1,0:T(8,128)(2,1)S(1)}) %tuple.25), branch_computations={%region_2.3_spmd, %region_3.4_spmd} | conditional | flops 229379 | bytes 1769518 | solution.py:195
  45.3 6.1 %all-gather = bf16[6,128,128]{2,1,0:T(8,128)(2,1)S(1)} all-gather(bf16[3,128,128]{2,1,0:T(8,128)(2,1)S(1)} %get-tuple-element.19), channel_id=2, replica_groups=mesh['zf'=4,'zb'=2,'za'=2,'core'=2,'tensor'=8,'guidance'=2] {'guidance'}, dimensions={0}, use_global_device_ids=true | all-gather | bytes 294912 | tf_op jit(solution)/shard_map/cond/branch_1_fun/all_gather | solution.py:225
  51.4 9.3 %all-gather.1 = bf16[8,1,128,128]{3,2,1,0:T(8,128)(2,1)S(1)} all-gather(bf16[2,1,128,128]{3,2,1,0:T(8,128)(2,1)S(1)} %fusion.2), channel_id=3, replica_groups=mesh['zf'=4,'zb'=2,'za'=2,'core'=2,'tensor'=8,'guidance'=2] {'za','core'}, dimensions={0}, use_global_device_ids=true | all-gather | bytes 327680 | tf_op jit(solution)/shard_map/cond/branch_1_fun/all_gather | solution.py:230
  60.7 0.0 collective-permute-done.2.far_ref
  60.7 0.0 collective-permute-done.3.mid_ref
  60.8 0.0 copy-done.2
  60.8 0.0 copy-done.3
  60.8 2.3 %shard_map.65 = bf16[8,144,128]{2,1,0:T(8,128)(2,1)S(1)} custom-call(bf16[4,2,128,128]{3,2,1,0:T(8,128)(2,1)S(1)} %get-tuple-element.30.query_ref, bf16[2,3,128,128]{3,2,1,0:T(8,128)(2,1)S(1)} %get-tuple-element.31.fresh_ref, bf16[2,128,256]{2,1,0:T(8,128)(2,1)S(1)} %bitcast.12, bf16[2,128,256]{2,1,0:T(8,128)(2,1)S(1)} %collective-permute-done.2.far_ref, ...), custom_call_target="tpu_custom_call" | custom-call | tf_op jit(solution)/shard_map/pallas_call | solution.py:178
  63.1 12.9 %all_to_all.15.reply_ref = bf16[8,144,128]{2,1,0:T(8,128)(2,1)S(1)} all-to-all(bf16[8,144,128]{2,1,0:T(8,128)(2,1)S(1)} %shard_map.65), channel_id=1, replica_groups=mesh['zf'=4,'zb'=2,'za'=2,'core'=2,'tensor'=8,'guidance'=2] {'guidance',..., dimensions={0} | all-to-all | bytes 589824 | tf_op jit(solution)/shard_map/all_to_all | solution.py:236
  76.0 0.0 copy-done.1
  76.0 0.0 copy-done.5
  76.0 0.0 copy-start.4
  76.0 1.2 %shard_map.66 = bf16[8,128,384]{2,1,0:T(8,128)(2,1)S(1)} custom-call(bf16[8,144,128]{2,1,0:T(8,128)(2,1)S(1)} %all_to_all.15.reply_ref, f32[3,2,3072]{2,1,0:T(2,128)S(1)} %copy-done.5, bf16[128,3072]{1,0:T(8,128)(2,1)S(1)} %copy-done.1), custom_call_target="tpu_custom_call" | custom-call | tf_op jit(solution)/shard_map/pallas_call | solution.py:178
  77.2 14.5 %all_to_all.16.parts_ref = bf16[8,128,384]{2,1,0:T(8,128)(2,1)S(1)} all-to-all(bf16[8,128,384]{2,1,0:T(8,128)(2,1)S(1)} %shard_map.66), channel_id=1, replica_groups=mesh['zf'=4,'zb'=2,'za'=2,'core'=2,'tensor'=8,'guidance'=2] {'tensor'}, dimensions={0} | all-to-all | bytes 1572864 | tf_op jit(solution)/shard_map/all_to_all | solution.py:238
  91.7 0.1 shard_map.67
  91.8 5.6 %all-gather.3 = bf16[256,384]{1,0:T(8,128)(2,1)S(1)} all-gather(bf16[128,384]{1,0:T(8,128)(2,1)S(1)} %shard_map.67), channel_id=5, replica_groups=mesh['zf'=4,'zb'=2,'za'=2,'core'=2,'tensor'=8,'guidance'=2] {'guidance'}, dimensions={0}, use_global_device_ids=true | all-gather | bytes 294912 | tf_op jit(solution)/shard_map/all_gather | solution.py:239
  97.5 0.0 copy-done.4
  97.5 0.7 shard_map.68
  (4 shorter events, 0.1 us)
Async XLA Ops:
  8.7 31.0 %collective-permute-start = (bf16[2,2,128,256]{3,2,1,0:T(8,128)(2,1)S(1)}, bf16[2,2,128,256]{3,2,1,0:T(8,128)(2,1)S(1)}, u32[]{:S(2)}, u32[]{:S(2)}) collective-permute-start(bf16[2,2,128,256]{3,2,1,0:T(8,128)(2,1)S(1)} %bitcast.15), channel_id=1, source_target_pairs={{0,128},{16,400},{128,256},{144,16},{256,384},{272,144},{384,0},{4... | collective-permute-start | bytes 786440 | tf_op jit(solution)/shard_map/ppermute | solution.py:208
  15.8 23.9 %collective-permute-start.1 = (bf16[2,2,128,256]{3,2,1,0:T(8,128)(2,1)S(1)}, bf16[2,2,128,256]{3,2,1,0:T(8,128)(2,1)S(1)}, u32[]{:S(2)}, u32[]{:S(2)}) collective-permute-start(bf16[2,2,128,256]{3,2,1,0:T(8,128)(2,1)S(1)} %bitcast.16), channel_id=1, source_target_pairs={{0,64},{16,464},{64,128},{80,16},{128,192},{144,80},{192,256},{208... | collective-permute-start | bytes 786440 | tf_op jit(solution)/shard_map/ppermute | solution.py:209
  20.1 17.9 %copy-start = (bf16[3,3072,128]{2,1,0:T(8,128)(2,1)S(1)}, bf16[3,3072,128]{2,1,0:T(8,128)(2,1)}, u32[]{:S(2)}) copy-start(bf16[3,3072,128]{2,1,0:T(8,128)(2,1)} %get-tuple-element.35.w_ref) | copy-start | bytes 7077892 | tf_op jit(solution)/shard_map/cond
  20.1 17.9 %copy-start.6 = (f32[3,2,3072]{2,1,0:T(2,128)S(1)}, f32[3,2,3072]{2,1,0:T(2,128)}, u32[]{:S(2)}) copy-start(f32[3,2,3072]{2,1,0:T(2,128)} %get-tuple-element.16.mod_ref) | copy-start | bytes 221188 | tf_op jit(solution)/shard_map/cond
  39.7 21.1 %copy-start.2 = (bf16[2,1,128,256]{3,2,1,0:T(8,128)(2,1)S(1)}, bf16[2,1,128,256]{3,2,1,0:T(8,128)(2,1)}, u32[]{:S(2)}) copy-start(bf16[2,1,128,256]{3,2,1,0:T(8,128)(2,1)} %param.14) | copy-start | bytes 393220
  39.7 21.1 %copy-start.3 = (bf16[2,1,256,256]{3,2,1,0:T(8,128)(2,1)S(1)}, bf16[2,1,256,256]{3,2,1,0:T(8,128)(2,1)}, u32[]{:S(2)}) copy-start(bf16[2,1,256,256]{3,2,1,0:T(8,128)(2,1)} %param.15) | copy-start | bytes 786436
  39.7 21.0 %collective-permute-start.3 = (bf16[2,2,128,256]{3,2,1,0:T(8,128)(2,1)S(1)}, bf16[2,2,128,256]{3,2,1,0:T(8,128)(2,1)S(1)}, u32[]{:S(2)}, u32[]{:S(2)}) collective-permute-start(bf16[2,2,128,256]{3,2,1,0:T(8,128)(2,1)S(1)} %collective-permute-done.near_ref), channel_id=1, source_target_pairs={{0,64},{16,464},{64,128},{80,16},{128,192},{144,80},{192,256},{208... | collective-permute-start | bytes 786440 | tf_op jit(solution)/shard_map/ppermute | solution.py:221
  42.3 18.4 %collective-permute-start.2 = (bf16[2,128,256]{2,1,0:T(8,128)(2,1)S(1)}, bf16[2,128,256]{2,1,0:T(8,128)(2,1)S(1)}, u32[]{:S(2)}, u32[]{:S(2)}) collective-permute-start(bf16[2,128,256]{2,1,0:T(8,128)(2,1)S(1)} %dynamic-slice_bitcast_fusion), channel_id=1, source_target_pairs={{0,128},{16,400},{128,256},{144,16},{256,384},{272,144},{384,0},{4... | collective-permute-start | bytes 393224 | tf_op jit(solution)/shard_map/ppermute | solution.py:222
  45.2 30.8 %copy-start.1 = (bf16[128,3072]{1,0:T(8,128)(2,1)S(1)}, bf16[128,3072]{1,0:T(8,128)(2,1)}, u32[]{:S(2)}) copy-start(bf16[128,3072]{1,0:T(8,128)(2,1)} %w_ref.1) | copy-start | bytes 2359300
  45.2 30.8 %copy-start.5 = (f32[3,2,3072]{2,1,0:T(2,128)S(1)}, f32[3,2,3072]{2,1,0:T(2,128)}, u32[]{:S(2)}) copy-start(f32[3,2,3072]{2,1,0:T(2,128)} %mod_ref.1) | copy-start | bytes 221188
  76.0 21.5 %copy-start.4 = (bf16[128,384]{1,0:T(8,128)(2,1)S(1)}, bf16[128,384]{1,0:T(8,128)(2,1)}, u32[]{:S(2)}) copy-start(bf16[128,384]{1,0:T(8,128)(2,1)} %tokens_ref.1) | copy-start | bytes 294916
